TPU v7x, 512 devices: a whole 4x4x16 slice. The times are simulated.
512 devices in a mesh: seq: 32 (over z, core), exp: 16 (over y, x).
Axes of the slice: x: 4, y: 4, z: 16, core: 2. Of those that a mesh axis runs over, the one named last changes fastest.
Arguments:
- queries: bfloat16 [4096, 64, 576], P('seq', 'exp'), may hold values from -16 to 16
- latents: bfloat16 [4096, 576], P('seq'), may hold values from -4.5 to 4.5
- cache: bfloat16 [512, 576], P('seq'), may hold values from -4 to 4
- prefix_len: int32 [1], replicated, may hold values from 256 to 512
- value_up: bfloat16 [64, 512, 128], P('exp'), may hold values from -2.5 to 2.5
- out_proj: bfloat16 [8192, 7168], P('exp', 'seq'), may hold values from -0.0625 to 0.0625
- residual: bfloat16 [4096, 7168], P('exp', 'seq'), may hold values from -24 to 24
- norm_gain: float32 [7168], P('seq'), may hold values from 0.25 to 1.75
- w_gate: bfloat16 [16, 7168, 2048], P('exp', 'seq'), may hold values from -0.0625 to 0.0625
- w_up: bfloat16 [16, 7168, 2048], P('exp', 'seq'), may hold values from -0.0625 to 0.0625
- w_down: bfloat16 [16, 2048, 7168], P('exp', None, 'seq'), may hold values from -0.125 to 0.125
- routes: int32 [4096, 8], replicated, may hold values from 0 to 255, as said below
- route_weights: bfloat16 [4096, 8], replicated, may hold values from 0.5 to 2
Outputs:
- layer_out: bfloat16 [4096, 7168], P('exp', 'seq')
Inputs may be any that keep to these rules, and one draw needn't show every extreme that they name: `routes`: each row names 8 different expert ids. Of the tokens of one aligned block of 256 rows, at most 32 name one held expert (0 to 15); over all tokens, at most 192 name one held expert. Both bounds are reached.
All inputs are finite; a program needn't handle non-finite values.
Results may differ from a plain program's by a relative error of at most 0.02.
Values may be sent and summed in bfloat16 or wider, within the bound.
A program may use at most 64 MiB of HBM per device.

v0:
```python
import jax
import jax.numpy as jnp
from jax import lax
from jax.sharding import PartitionSpec as P

D = 7168
LAT = 512
ROPE = 64
QK_NOPE = 128
VHEAD = 128
SRC_CAP = 32


eps = 1e-06
floor_score = -1e30


def absorb(state, query_rows, visible, piece, scale):
    best, total, summed = state
    scores = jnp.einsum("rc,kc->rk", query_rows, piece, preferred_element_type=jnp.float32) * scale
    scores = jnp.where(visible, scores, floor_score)
    newest = jnp.maximum(best, jnp.max(scores, axis=1))
    weights = jnp.where(visible, jnp.exp(scores - newest[:, None]), 0.0)
    fade = jnp.exp(best - newest)
    total = total * fade + jnp.sum(weights, axis=1)
    summed = summed * fade[:, None] + jnp.dot(
        weights.astype(jnp.bfloat16), piece[:, :LAT], preferred_element_type=jnp.float32
    )
    return (newest, total, summed)


def local(
    queries,
    latents,
    cache,
    prefix_len,
    value_up,
    out_proj,
    residual,
    norm_gain,
    w_gate,
    w_up,
    w_down,
    routes,
    route_weights,
):
    exp_count = lax.axis_size("exp")
    seq_index = lax.axis_index("seq")
    exp_index = lax.axis_index("exp")
    held_cap = SRC_CAP * min(exp_count, 6)
    tok_dev, heads_dev, qwidth = queries.shape
    scale = (QK_NOPE + ROPE) ** (-0.5)
    own_tokens = seq_index * tok_dev + jnp.arange(tok_dev, dtype=jnp.int32)
    row_count = tok_dev * heads_dev
    query_rows = queries.reshape(row_count, qwidth)
    row_token = jnp.repeat(own_tokens, heads_dev)
    state = (
        jnp.full((row_count,), floor_score, jnp.float32),
        jnp.zeros((row_count,), jnp.float32),
        jnp.zeros((row_count, LAT), jnp.float32),
    )
    live = prefix_len[0]
    piece = lax.all_gather(cache, "seq", axis=0, tiled=True)
    key_index = jnp.arange(piece.shape[0], dtype=jnp.int32)
    visible = jnp.broadcast_to((key_index < live)[None, :], (row_count, piece.shape[0]))
    state = lax.cond(
        jnp.int32(0) < live,
        lambda inner: absorb(inner, query_rows, visible, piece, scale),
        lambda inner: inner,
        state,
    )
    window_piece = lax.all_gather(latents, "seq", axis=0, tiled=True)
    key_index = jnp.arange(window_piece.shape[0], dtype=jnp.int32)
    seg_state = tuple((member for member in state))
    window_visible = key_index[None, :] <= row_token[:, None]
    parts = [
        lax.cond(
            jnp.int32(0) <= jnp.max(row_token),
            lambda inner: absorb(inner, query_rows, window_visible, window_piece, scale),
            lambda inner: inner,
            seg_state,
        )
    ]
    state = tuple((jnp.concatenate([part[slot] for part in parts], axis=0) for slot in range(3)))
    context = (state[2] / state[1][:, None]).astype(jnp.bfloat16).reshape(tok_dev, heads_dev, LAT)
    head_out = jnp.einsum(
        "thl,hlv->thv", context, value_up, preferred_element_type=jnp.float32
    ).astype(jnp.bfloat16)
    head_out = head_out.reshape(tok_dev, heads_dev * VHEAD)
    terms = jnp.dot(
        lax.all_gather(head_out, "seq", axis=0, tiled=True),
        out_proj,
        preferred_element_type=jnp.float32,
    ).astype(jnp.bfloat16)
    width_dev = terms.shape[1]
    summed_terms = lax.psum(terms.astype(jnp.float32).astype(jnp.bfloat16), "exp").astype(
        jnp.float32
    )
    every_row = lax.all_gather(residual, "exp", axis=0, tiled=True)
    hidden_all = every_row.astype(jnp.float32) + summed_terms
    squares = lax.psum(jnp.sum(hidden_all * hidden_all, axis=1), "seq")
    normed = (hidden_all * lax.rsqrt(squares / D + eps)[:, None] * norm_gain).astype(jnp.bfloat16)
    hit = routes == exp_index
    chosen = jnp.any(hit, axis=1)
    weight_all = jnp.sum(jnp.where(hit, route_weights.astype(jnp.float32), 0.0), axis=1)
    picked = jnp.nonzero(chosen, size=held_cap, fill_value=0)[0].astype(jnp.int32)
    valid = jnp.arange(held_cap, dtype=jnp.int32) < jnp.sum(chosen.astype(jnp.int32))
    row_weight = jnp.where(valid, weight_all[picked], 0.0)
    rows_in = normed[picked]
    gate_part = jnp.dot(rows_in, w_gate[0], preferred_element_type=jnp.float32)
    up_part = jnp.dot(rows_in, w_up[0], preferred_element_type=jnp.float32)
    gate_full = lax.psum(gate_part.astype(jnp.bfloat16), "seq").astype(jnp.float32)
    up_full = lax.psum(up_part.astype(jnp.bfloat16), "seq").astype(jnp.float32)
    inner = (jax.nn.silu(gate_full) * up_full).astype(jnp.bfloat16)
    produced = jnp.dot(inner, w_down[0], preferred_element_type=jnp.float32)
    weighted = (row_weight[:, None] * produced).astype(jnp.bfloat16)
    placed = (
        jnp.zeros((routes.shape[0], width_dev), jnp.float32)
        .at[picked]
        .add(weighted.astype(jnp.float32))
    )
    mixed = lax.psum_scatter(
        placed.astype(jnp.bfloat16), "exp", scatter_dimension=0, tiled=True
    ).astype(jnp.float32)
    block_rows = mixed.shape[0]
    own_hidden = lax.dynamic_slice_in_dim(hidden_all, exp_index * block_rows, block_rows, 0)
    result = (own_hidden + mixed).astype(jnp.bfloat16)
    return result


def solution(mesh):
    in_specs = (
        P("seq", "exp", None),
        P("seq", None),
        P("seq", None),
        P(),
        P("exp", None, None),
        P("exp", "seq"),
        P("exp", "seq"),
        P("seq"),
        P("exp", "seq", None),
        P("exp", "seq", None),
        P("exp", None, "seq"),
        P(),
        P(),
    )
    out_specs = P("exp", "seq")
    return jax.shard_map(local, mesh=mesh, in_specs=in_specs, out_specs=out_specs, check_vma=False)
```

profile of v0, /device:TPU:1, one launch (start us, length us, event | category | flops | bytes accessed | tf_op | source)
XLA Modules:
  0.0 798.1 jit_solution(5216129556427661612)
XLA Ops:
  6.5 1.8 copy.27
  8.3 0.0 all-gather.6.cloned.1.call-update
  8.3 0.0 all-gather.8.cloned.1.call-start
  8.4 1.6 copy.26
  10.0 0.3 reshape.87
  11.0 0.6 broadcast_reduce_fusion
  12.3 40.2 %all_gather.13 = bf16[512,576]{1,0:T(8,128)(2,1)S(1)} all-gather(bf16[16,576]{1,0:T(8,128)(2,1)} %param.19), channel_id=1, replica_groups=mesh['seq'=32,'exp'=16] {'seq'}, dimensions={0}, use_global_device_ids=true | all-gather | bytes 608256 | tf_op jit(solution)/shard_map/all_gather | solution.py:63
  52.5 4.7 conditional.2
  52.5 0.7 compare_reduce_fusion
  53.2 0.6 fusion.46
  53.8 0.6 exponential_multiply_fusion
  54.4 1.3 convolution_add_fusion
  55.6 0.9 fusion.20
  56.5 0.7 fusion.27
  57.2 33.8 %all-gather.6.cloned.1.call-done = bf16[4096,576]{1,0:T(8,128)(2,1)} async-done(((bf16[128,576]{1,0:T(8,128)(2,1)}), bf16[4096,576]{1,0:T(8,128)(2,1)}) %all-gather.6.cloned.1.call-update) | async-done | bytes 4718608 | tf_op jit(solution)/shard_map/all_gather | solution.py:72
  91.0 4.2 le.22
  95.3 15.5 %conditional.3 = ((f32[512]{0:T(512)S(1)}, f32[512,512]{1,0:T(8,128)S(1)})) conditional(s32[]{:T(128)} %convert_element_type.81, (f32[512]{0:T(512)S(1)}, f32[512,512]{1,0:T(8,128)S(1)}) %tuple.22, (s32[128]{0:T(128)S(1)}, s32[512,4096]{1,0:T(8,128)}, bf16[512,576]{1,0:T(8,128)(2,1)S(1)}, bf16[4096,576]{1,0:T(8,128)(2,1)}, f32[512]{0:T(512)}, ...), branch_computations={%region_5.6_spmd, %region_6.9_spmd} | conditional | flops 4593288192 | bytes 70357560 | solution.py:77
  95.3 0.1 broadcast_in_dim.74
  95.4 0.1 le.16
  95.5 8.3 %fusion = (f32[512]{0:T(512)S(1)}, pred[512,4096]{1,0:T(32,128)(4,1)S(1)}, f32[512,4096]{1,0:T(8,128)S(1)}) fusion(s32[512,4096]{1,0:T(8,128)} %get-tuple-element.45, s32[512]{0:T(512)S(1)} %le.16, bf16[512,576]{1,0:T(8,128)(2,1)S(1)} %get-tuple-element.47, bf16[4096,576]{1,0:T(8,128)(2,1)} %get-tuple-element.48), kind=kOutput, calls=%fused_computation.6 | convolution fusion | flops 2424307200 | bytes 24186880 | tf_op jit(solution)/shard_map/cond/branch_1_fun/rc,kc->rk/dot_general | solution.py:20
  103.8 0.7 max.2
  104.5 2.8 fusion.2
  107.3 0.7 multiply_add_fusion
  107.9 2.9 fusion.10
  110.8 0.1 divide_convert_fusion
  111.0 0.1 reshape.88
  111.1 1.0 convolution_convert_fusion.3
  112.1 0.0 all-gather.4.cloned.1.call-start
  112.2 0.7 all-gather.4.cloned.1.call-update
  112.9 0.2 all-reduce.5.cloned.1.call-start
  113.1 0.1 select_reduce_fusion
  113.2 0.3 reduce-window.16
  113.5 0.1 slice.29
  113.6 0.1 reduce-window.19
  113.7 0.1 slice_reduce_fusion
  113.8 75.0 %all-gather.8.cloned.1.call-done = bf16[4096,512]{0,1:T(8,128)(2,1)} async-done(((bf16[128,512]{0,1:T(8,128)(2,1)}), bf16[4096,512]{0,1:T(8,128)(2,1)}) %all-gather.8.cloned.1.call-update) | async-done | bytes 4194320 | tf_op jit(solution)/shard_map/all_gather | solution.py:91
  188.8 4.7 convolution_convert_fusion
  193.5 0.0 all-reduce.7.cloned.1.call-start
  193.6 0.1 broadcast_add_fusion
  193.7 28.8 %scatter_custom_fusion = s32[192]{0:T(256)S(1)} fusion(s32[4096]{0:T(1024)S(1)} %bitcast.33, s32[4096]{0:T(1024)S(1)} %broadcast.76, s32[]{:T(128)} %constant.58.clone.1), kind=kCustom, calls=%fused_computation.82 | custom fusion | flops 4096 | bytes 772 | tf_op jit(solution)/shard_map/scatter-add | solution.py:106
  222.5 0.3 reduce-window.24
  222.8 0.1 slice.23
  222.9 0.1 slice_reduce_fusion.1
  223.0 0.6 convert_reduce_fusion
  223.7 0.1 add_bitcast_fusion
  223.7 0.7 compare_select_fusion.1
  224.4 24.4 %all-gather.4.cloned.1.call-done = bf16[4096,224]{0,1:T(8,128)(2,1)} async-done(((bf16[256,224]{0,1:T(8,128)(2,1)}), bf16[4096,224]{0,1:T(8,128)(2,1)}) %all-gather.4.cloned.1.call-update) | async-done | bytes 1835024 | tf_op jit(solution)/shard_map/all_gather | solution.py:99
  248.8 122.4 %all-reduce.5.cloned.1.call-done = bf16[4096,224]{0,1:T(8,128)(2,1)} async-done(((bf16[4096,224]{0,1:T(8,128)(2,1)}), bf16[4096,224]{0,1:T(8,128)(2,1)}) %all-reduce.5.cloned.1.call-update) | async-done | bytes 1835024 | tf_op jit(solution)/shard_map/psum | solution.py:96
  371.2 4.5 convert_add_fusion
  375.7 90.6 %psum.29 = f32[4096]{0:T(1024)S(1)} all-reduce(f32[4096]{0:T(1024)S(1)} %get-tuple-element.74), channel_id=1, replica_groups=mesh['seq'=32,'exp'=16] {'seq'}, use_global_device_ids=true, to_apply=%region_19.20 | all-reduce | flops 4096 | bytes 32768 | tf_op jit(solution)/shard_map/psum | solution.py:101
  466.3 3.5 multiply_convert_fusion
  469.8 3.2 copy.30
  473.1 1.0 gather_fusion.1
  474.1 1.3 convolution_convert_fusion.1
  475.3 2.4 convolution_convert_fusion.2
  477.8 0.0 reduce-scatter.2.cloned.1.call-start
  477.9 1.4 gather_fusion
  479.3 0.7 compare_select_fusion.4
  480.0 211.5 %all-reduce.7.cloned.1.call-done = (bf16[192,2048]{1,0:T(8,128)(2,1)}, bf16[192,2048]{1,0:T(8,128)(2,1)}) async-done(((bf16[192,2048]{1,0:T(8,128)(2,1)}, bf16[192,2048]{1,0:T(8,128)(2,1)}), (bf16[192,2048]{1,0:T(8,128)(2,1)}, bf16[192,2048]{1,0:T(8,128)(2,1)})) %all-reduce.7.cloned.1.call-update) | async-done | bytes 1572880 | tf_op jit(solution)/shard_map/psum | solution.py:113
  691.5 2.0 fusion.36
  693.5 3.9 scatter_custom_fusion.1
  697.4 4.6 copy.31
  702.1 87.5 %reduce-scatter.2.cloned.1.call-done = bf16[256,224]{0,1:T(8,128)(2,1)} async-done(((bf16[4096,224]{0,1:T(8,128)(2,1)}), bf16[256,224]{0,1:T(8,128)(2,1)}) %reduce-scatter.2.cloned.1.call-update) | async-done | bytes 114704 | tf_op jit(solution)/shard_map/reduce_scatter | solution.py:122
  789.6 1.7 add_convert_fusion
  (31 shorter events, 0.2 us)
Async XLA Ops:
  6.5 467.5 %copy-start = (bf16[1,224,2048]{2,1,0:T(8,128)(2,1)S(1)}, bf16[1,224,2048]{2,1,0:T(8,128)(2,1)}, u32[]{:S(2)}) copy-start(bf16[1,224,2048]{2,1,0:T(8,128)(2,1)} %param.26) | copy-start | bytes 2752516
  6.5 84.5 %all-gather.6.cloned.1.call-start = ((), (), s32[]{:S(2)}) async-start(), calls=%async_computation.2 | async-start | bytes 5406720 | tf_op jit(solution)/shard_map/all_gather | solution.py:72
  8.3 180.5 %all-gather.8.cloned.1.call-start = ((), (), s32[]{:S(2)}) async-start(), calls=%async_computation.3 | async-start | bytes 4325376 | tf_op jit(solution)/shard_map/all_gather | solution.py:91
  95.3 15.8 %copy-start.2 = (bf16[4,512,128]{2,1,0:T(8,128)(2,1)S(1)}, bf16[4,512,128]{2,1,0:T(8,128)(2,1)}, u32[]{:S(2)}) copy-start(bf16[4,512,128]{2,1,0:T(8,128)(2,1)} %param.21) | copy-start | bytes 1572868
  95.3 17.8 %copy-start.3 = (s32[4096,8]{0,1:T(8,128)S(1)}, s32[4096,8]{0,1:T(8,128)}, u32[]{:S(2)}) copy-start(s32[4096,8]{0,1:T(8,128)} %param.28) | copy-start | bytes 393220
  95.3 17.8 %copy-start.4 = (bf16[4096,8]{0,1:T(8,128)(2,1)S(1)}, bf16[4096,8]{0,1:T(8,128)(2,1)}, u32[]{:S(2)}) copy-start(bf16[4096,8]{0,1:T(8,128)(2,1)} %param.29) | copy-start | bytes 196612
  104.5 3.5 copy-start.6
  112.1 136.6 %all-gather.4.cloned.1.call-start = ((), (), s32[]{:S(2)}) async-start(), calls=%async_computation.1 | async-start | bytes 1949696 | tf_op jit(solution)/shard_map/all_gather | solution.py:99
  112.9 258.3 %all-reduce.5.cloned.1.call-start = ((), (), s32[]{:S(2)}) async-start(), calls=%async_computation.4 | async-start | bytes 3670016 | tf_op jit(solution)/shard_map/psum | solution.py:96
  193.5 272.8 %copy-start.5 = (f32[224]{0:T(256)S(1)}, f32[224]{0:T(256)}, u32[]{:S(2)}) copy-start(f32[224]{0:T(256)} %param.24) | copy-start | bytes 2692
  193.5 497.9 %all-reduce.7.cloned.1.call-start = ((), (), s32[]{:S(2)}) async-start(), calls=%async_computation.6 | async-start | bytes 3145728 | tf_op jit(solution)/shard_map/psum | solution.py:113
  248.8 217.6 %copy-start.1 = (bf16[4096,224]{0,1:T(8,128)(2,1)S(1)}, bf16[4096,224]{0,1:T(8,128)(2,1)}, u32[]{:S(2)}) copy-start(bf16[4096,224]{0,1:T(8,128)(2,1)} %all-gather.4.cloned.1.call-done) | copy-start | bytes 5505028
  474.1 217.4 %copy-start.7 = (bf16[1,2048,224]{1,2,0:T(8,128)(2,1)S(1)}, bf16[1,2048,224]{1,2,0:T(8,128)(2,1)}, u32[]{:S(2)}) copy-start(bf16[1,2048,224]{1,2,0:T(8,128)(2,1)} %param.27) | copy-start | bytes 2752516
  477.8 311.8 %reduce-scatter.2.cloned.1.call-start = ((), (), s32[]{:S(2)}) async-start(), calls=%async_computation.5 | async-start | bytes 1949696 | tf_op jit(solution)/shard_map/reduce_scatter | solution.py:122
Sparse Core Ops, SparseCore 0:
  9.5 81.5 all-gather.5
  112.3 76.4 all-gather.7
  191.8 56.9 all-gather.3
  252.0 119.1 all-reduce.4
  477.9 213.5 all-reduce.6
  702.2 87.3 reduce-scatter.1
where the time goes:
time: 799 us; the launch traced here: 798 us
  waiting for transfers between devices  555 us (69%)
  blocking collectives  131 us (16%)
  other arithmetic  53.1 us (7%)
  matrix products  24.4 us (3%)
  local copies, waits for them, and re-layouts  18.9 us (2%)
  between operations  15 us (2%)
    psum x1, waiting for transfers between devices, local(): up_full = lax.psum(up_part.astype(jnp.bfloat16), 'seq').astype(jnp.float32)  212 us
    psum x1, waiting for transfers between devices, local(): lax.psum(terms.astype(jnp.float32).astype(jnp.bfloat16), 'exp')  122 us
    psum x1, blocking collectives, local(): squares = lax.psum(jnp.sum(hidden_all * hidden_all, axis=1), 'seq')  90.6 us
    reduce_scatter x1, waiting for transfers between devices, local(): lax.psum_scatter(placed.astype(jnp.bfloat16), 'exp', scatter_dimension=0,...  87.5 us
    all_gather x1, waiting for transfers between devices, local(): lax.all_gather(head_out, 'seq', axis=0, tiled=True)  75 us
    all_gather x1, blocking collectives, local(): piece = lax.all_gather(cache, 'seq', axis=0, tiled=True)  40.2 us
    all_gather x1, waiting for transfers between devices, local(): window_piece = lax.all_gather(latents, 'seq', axis=0, tiled=True)  33.8 us
    scatter-add x1, other arithmetic, local(): jnp.nonzero(chosen, size=held_cap, fill_value=0)[0].astype(jnp.int32)  28.8 us
  transfers between devices with their start and end apart: 6, of which 6 were waited for; matrix products, arithmetic and copies ran while one was open for 6% of the time, Pallas kernels for 0%

commit v1 on v0

v1 whole, which is shorter than its diff:
```python
import functools

import jax
import jax.numpy as jnp
from jax import lax
from jax.experimental import pallas as pl
from jax.experimental.pallas import tpu as pltpu
from jax.sharding import PartitionSpec as P

LAT = 512
ROPE = 64
QK_NOPE = 128
SRC_CAP = 32

EPS = 1e-06
FLOOR = -1e30
SCALE = (QK_NOPE + ROPE) ** (-0.5)
MESH = pl.DeviceIdType.MESH
VMEM = pltpu.VMEM
VMEM_BYTES = 48 * 1024 * 1024


def rdot(a, b):
    return jnp.dot(a, b, preferred_element_type=jnp.float32)


def rdot_t(a, b):
    return lax.dot_general(
        a, b, (((1,), (1,)), ((), ())), preferred_element_type=jnp.float32
    )


def place(zs):
    s = lax.axis_index("seq")
    z, c = s // 2, lax.rem(s, 2)
    above = lax.rem(z + 1, zs) * 2 + c
    below = lax.rem(z + zs - 1, zs) * 2 + c
    twin = 2 * z + 1 - c
    return z, c, above, below, twin


def greet(zs, peers):
    _, _, above, below, twin = place(zs)
    e = lax.axis_index("exp")
    barrier = pltpu.get_barrier_semaphore()
    for to in (above, below, twin):
        pl.semaphore_signal(
            barrier, inc=1, device_id={"seq": to, "exp": e}, device_id_type=MESH
        )
    if peers > 1:
        s = lax.axis_index("seq")

        def hello(j, carry):
            pl.semaphore_signal(
                barrier,
                inc=1,
                device_id={"seq": s, "exp": lax.rem(e + j, peers)},
                device_id_type=MESH,
            )
            return carry

        lax.fori_loop(1, peers, hello, 0)
    pl.semaphore_wait(barrier, 3 + max(peers - 1, 0))


def ring_sems(zs):
    up, down = zs // 2, zs // 2 - 1
    dma = pltpu.SemaphoreType.DMA
    return [dma((up,)), dma((up,)), dma((down,)), dma((down,)), dma((zs,)), dma((zs,))]


def ring_gather(zs, buf, sems, own, visit):
    us, ur, ds, dr, ts, tr = sems
    up, down = zs // 2, zs // 2 - 1
    z, c, above, below, twin = place(zs)
    e = lax.axis_index("exp")

    def copy(zb, core, ssem, rsem, to):
        slot = buf.at[2 * zb + core]
        return pltpu.make_async_remote_copy(
            src_ref=slot,
            dst_ref=slot,
            send_sem=ssem,
            recv_sem=rsem,
            device_id={"seq": to, "exp": e},
            device_id_type=MESH,
        )

    def lower(k):
        return lax.rem(z - k + zs, zs)

    def upper(k):
        return lax.rem(z + k, zs)

    copy(z, c, us.at[0], ur.at[0], above).start()
    copy(z, c, ds.at[0], dr.at[0], below).start()
    copy(z, c, ts.at[0], tr.at[0], twin).start()

    def step(k, carry):
        @pl.when(k <= up)
        def _():
            copy(lower(k), c, us.at[k - 1], ur.at[k - 1], above).wait_recv()

            @pl.when(k < up)
            def _():
                copy(lower(k), c, us.at[k], ur.at[k], above).start()

            copy(lower(k), c, ts.at[k], tr.at[k], twin).start()

        @pl.when(k <= down)
        def _():
            copy(upper(k), c, ds.at[k - 1], dr.at[k - 1], below).wait_recv()

            @pl.when(k < down)
            def _():
                copy(upper(k), c, ds.at[k], dr.at[k], below).start()

            copy(upper(k), c, ts.at[up + k], tr.at[up + k], twin).start()

        @pl.when(k == 1)
        def _():
            copy(z, 1 - c, ts.at[0], tr.at[0], twin).wait_recv()
            own()

        def side(which, inner):
            j = k - 1

            @pl.when((which == 0) | (j <= down))
            def _():
                zb = lax.rem(z + jnp.where(which == 0, zs - j, j), zs)
                index = jnp.where(which == 0, j, up + j)
                copy(zb, 1 - c, ts.at[index], tr.at[index], twin).wait_recv()
                visit(zb)

            return inner

        @pl.when(k > 1)
        def _():
            lax.fori_loop(0, 2, side, 0)

        return carry

    lax.fori_loop(1, up + 2, step, 0)

    def drain(k, carry):
        copy(lower(k), c, us.at[k], ur.at[k], above).wait_send()
        copy(lower(k), c, ts.at[k], tr.at[k], twin).wait_send()

        @pl.when(k < down)
        def _():
            copy(upper(k), c, ds.at[k], dr.at[k], below).wait_send()
            copy(upper(k), c, ts.at[up + 1 + k], tr.at[up + 1 + k], twin).wait_send()

        return carry

    lax.fori_loop(0, up, drain, 0)
    copy(lower(up), c, ts.at[up], tr.at[up], twin).wait_send()


def attention_kernel(
    zs, q_ref, lat_ref, cache_ref, live_ref, vup_ref, out_ref, buf, best, total, acc, *sems
):
    tok = lat_ref.shape[0]
    slots = cache_ref.shape[0]
    rows, width = q_ref.shape
    heads = rows // tok
    z, c, _, _, _ = place(zs)
    s = 2 * z + c
    greet(zs, 0)
    buf[s, 0:tok, :] = lat_ref[...]
    buf[s, tok : tok + slots, :] = cache_ref[...]

    def absorb(keys, visible, first):
        scores = rdot_t(q_ref[...], keys) * SCALE
        if visible is not None:
            scores = jnp.where(visible, scores, FLOOR)
        top = jnp.max(scores, axis=1, keepdims=True)
        if first:
            newest = top
            weights = jnp.exp(scores - newest)
            total[...] = jnp.sum(weights, axis=1, keepdims=True)
            acc[...] = rdot(weights.astype(jnp.bfloat16), keys[:, :LAT])
        else:
            before = best[...]
            newest = jnp.maximum(before, top)
            fade = jnp.exp(before - newest)
            weights = jnp.exp(scores - newest)
            total[...] = total[...] * fade + jnp.sum(weights, axis=1, keepdims=True)
            acc[...] = acc[...] * fade + rdot(weights.astype(jnp.bfloat16), keys[:, :LAT])
        best[...] = newest

    def pair(zb):
        return buf[pl.ds(2 * zb, 2), 0:tok, :].reshape(2 * tok, width)

    def own():
        row = lax.broadcasted_iota(jnp.int32, (rows, 2 * tok), 0)
        key = lax.broadcasted_iota(jnp.int32, (rows, 2 * tok), 1)
        absorb(pair(z), key <= lax.rem(row, tok) + c * tok, True)

    def visit(zb):
        @pl.when(zb < z)
        def _():
            absorb(pair(zb), None, False)

    ring_gather(zs, buf, sems, own, visit)

    live = live_ref[0]
    group = max(1, min(256, slots * 2 * zs) // slots)

    def prefix(i, carry):
        keys = buf[pl.ds(i * group, group), tok : tok + slots, :].reshape(group * slots, width)
        key = lax.broadcasted_iota(jnp.int32, (rows, group * slots), 1) + i * (group * slots)
        absorb(keys, key < live, False)
        return carry

    lax.fori_loop(0, 2 * zs // group, prefix, 0)

    for h in range(heads):
        part = pl.ds(h * tok, tok)
        context = (acc[part, :] / total[part, :]).astype(jnp.bfloat16)
        vh = vup_ref.shape[2]
        out_ref[:, h * vh : (h + 1) * vh] = rdot(context, vup_ref[h]).astype(jnp.bfloat16)


def project_kernel(zs, peers, head_ref, proj_ref, out_ref, buf, terms, got, t_send, t_recv, *sems):
    tok, inner = head_ref.shape
    width = proj_ref.shape[1]
    z, c, _, _, _ = place(zs)
    s = 2 * z + c
    e = lax.axis_index("exp")
    greet(zs, peers)
    buf[s] = head_ref[...]

    def hand(zb):
        return pltpu.make_async_remote_copy(
            src_ref=terms.at[zb],
            dst_ref=got.at[e],
            send_sem=t_send.at[zb],
            recv_sem=t_recv.at[e],
            device_id={"seq": s, "exp": zb},
            device_id_type=MESH,
        )

    def visit(zb):
        rows = buf[pl.ds(2 * zb, 2)].reshape(2 * tok, inner)
        terms[zb] = rdot(rows, proj_ref[...]).astype(jnp.bfloat16)

        @pl.when(zb != e)
        def _():
            hand(zb).start()

    ring_gather(zs, buf, sems, lambda: visit(z), visit)
    out_ref[...] = terms[e].astype(jnp.float32)

    def collect(j, carry):
        g = lax.rem(e + j, peers)
        pltpu.make_async_remote_copy(
            src_ref=terms.at[g],
            dst_ref=got.at[g],
            send_sem=t_send.at[g],
            recv_sem=t_recv.at[g],
            device_id={"seq": s, "exp": g},
            device_id_type=MESH,
        ).wait_recv()
        out_ref[...] += got[g].astype(jnp.float32)
        return carry

    lax.fori_loop(1, peers, collect, 0)

    def drain(j, carry):
        hand(lax.rem(e + j, peers)).wait_send()
        return carry

    lax.fori_loop(1, peers, drain, 0)


def swap_exp(peers, send, recv, s_sem, r_sem):
    s = lax.axis_index("seq")
    e = lax.axis_index("exp")

    def copy(j, to, slot):
        return pltpu.make_async_remote_copy(
            src_ref=send.at[to],
            dst_ref=recv.at[slot],
            send_sem=s_sem.at[j],
            recv_sem=r_sem.at[j],
            device_id={"seq": s, "exp": to},
            device_id_type=MESH,
        )

    def start(j, carry):
        copy(j, lax.rem(e + j, peers), e).start()
        return carry

    lax.fori_loop(1, peers, start, 0)
    recv[e] = send[e]

    def finish(j, carry):
        copy(j, lax.rem(e + j, peers), lax.rem(e + peers - j, peers)).wait_recv()
        return carry

    lax.fori_loop(1, peers, finish, 0)

    def drain(j, carry):
        copy(j, lax.rem(e + j, peers), e).wait_send()
        return carry

    lax.fori_loop(1, peers, drain, 0)


def split_rows(v):
    row = lax.broadcasted_iota(jnp.int32, v.shape, 0)
    high = v.astype(jnp.bfloat16).astype(jnp.float32)
    rest = v - high
    mid = rest.astype(jnp.bfloat16).astype(jnp.float32)
    low = rest - mid
    parts = jnp.where(row == 0, high, jnp.where(row == 1, mid, jnp.where(row == 2, low, 0.0)))
    return parts.astype(jnp.bfloat16)


def join_rows(block):
    return jnp.sum(block.astype(jnp.float32), axis=0, keepdims=True)


def experts_kernel(
    zs,
    peers,
    features,
    att_ref,
    res_ref,
    gain_ref,
    pick_ref,
    mix_ref,
    pack_ref,
    unpack_ref,
    wg_ref,
    wu_ref,
    wd_ref,
    out_ref,
    hid,
    d_send,
    d_recv,
    xs,
    sqv,
    mine,
    other,
    theirs,
    up_out,
    up_in,
    dn_out,
    dn_in,
    ibuf,
    acc,
    c_send,
    c_recv,
    ds_sem,
    dr_sem,
    ps_sem,
    pr_sem,
    us_sem,
    ur_sem,
    ls_sem,
    lr_sem,
    cs_sem,
    cr_sem,
    *sems,
):
    tokens, width = res_ref.shape
    wide = hid.shape[1]
    cap = pack_ref.shape[0]
    half = cap // 2
    cols = ibuf.shape[2]
    up, down = zs // 2, zs // 2 - 1
    z, c, above, below, twin = place(zs)
    e = lax.axis_index("exp")
    greet(zs, peers)

    hid[...] = jnp.zeros_like(hid)
    hid[:, 0:width] = res_ref[...].astype(jnp.float32) + att_ref[...]
    hidden = hid[...]
    squares = jnp.sum(hidden * hidden, axis=1, keepdims=True)
    high = squares.astype(jnp.bfloat16).astype(jnp.float32)
    rest = squares - high
    mid = rest.astype(jnp.bfloat16).astype(jnp.float32)
    low = rest - mid
    lane = lax.broadcasted_iota(jnp.int32, (tokens, wide), 1)
    ext = jnp.where(
        lane < width,
        hidden * gain_ref[...],
        jnp.where(
            lane == width,
            high,
            jnp.where(lane == width + 1, mid, jnp.where(lane == width + 2, low, 0.0)),
        ),
    ).astype(jnp.bfloat16)
    d_send[...] = rdot(pick_ref[...], ext).astype(jnp.bfloat16).reshape(d_send.shape)
    swap_exp(peers, d_send, d_recv, ds_sem, dr_sem)

    arrived = d_recv[...].reshape(peers * SRC_CAP, wide)
    packed = rdot(pack_ref[...], arrived).astype(jnp.bfloat16)
    xs[...] = packed
    mark = lax.broadcasted_iota(jnp.int32, (16, wide), 1)
    ones = jnp.where((mark >= width) & (mark < width + 3), 1.0, 0.0).astype(jnp.bfloat16)
    sqv[...] = jnp.zeros_like(sqv)
    sqv[:, 0:cap] = rdot_t(ones, packed)
    own_sq = sqv[...]
    tail = split_rows(own_sq)
    x_mine = xs[pl.ds(pl.multiple_of(c * half, 16), half), 0:width]
    x_other = xs[pl.ds(pl.multiple_of((1 - c) * half, 16), half), 0:width]

    def to_twin(d):
        return pltpu.make_async_remote_copy(
            src_ref=other.at[d],
            dst_ref=theirs.at[d],
            send_sem=ps_sem.at[d],
            recv_sem=pr_sem.at[d],
            device_id={"seq": twin, "exp": e},
            device_id_type=MESH,
        )

    def partial(i, carry):
        t = i // 2
        d = lax.rem(z + jnp.where(lax.rem(i, 2) == 0, up - t, zs - down + t), zs)
        span = pl.ds(pl.multiple_of(d * cols, cols), cols)
        other[d, 0:half, 0:cols] = rdot(x_other, wg_ref[:, span]).astype(jnp.bfloat16)
        other[d, 0:half, cols : 2 * cols] = rdot(x_other, wu_ref[:, span]).astype(jnp.bfloat16)
        other[d, half : half + 16, :] = tail
        to_twin(d).start()
        mine[d, :, 0:cols] = rdot(x_mine, wg_ref[:, span])
        mine[d, :, cols : 2 * cols] = rdot(x_mine, wu_ref[:, span])
        return carry

    lax.fori_loop(0, zs, partial, 0)

    def up_copy(t):
        return pltpu.make_async_remote_copy(
            src_ref=up_out.at[t],
            dst_ref=up_in.at[t],
            send_sem=us_sem.at[t],
            recv_sem=ur_sem.at[t],
            device_id={"seq": above, "exp": e},
            device_id_type=MESH,
        )

    def dn_copy(t):
        return pltpu.make_async_remote_copy(
            src_ref=dn_out.at[t],
            dst_ref=dn_in.at[t],
            send_sem=ls_sem.at[t],
            recv_sem=lr_sem.at[t],
            device_id={"seq": below, "exp": e},
            device_id_type=MESH,
        )

    def pair_sum(d):
        to_twin(d).wait_recv()
        body = mine[d] + theirs[d, 0:half, :].astype(jnp.float32)
        sq = own_sq + join_rows(theirs[d, half : half + 16, :])
        return body, sq

    def relay(d, out, into, copy, t, first):
        body, sq = pair_sum(d)
        if not first:
            copy(t - 1).wait_recv()
            body = body + into[t - 1, 0:half, :].astype(jnp.float32)
            sq = sq + join_rows(into[t - 1, half : half + 16, :])
        out[t, 0:half, :] = body.astype(jnp.bfloat16)
        out[t, half : half + 16, :] = split_rows(sq)
        copy(t).start()

    relay(lax.rem(z + up, zs), up_out, up_in, up_copy, 0, True)
    relay(lax.rem(z + zs - down, zs), dn_out, dn_in, dn_copy, 0, True)

    def ring(t, carry):
        relay(lax.rem(z + up - t, zs), up_out, up_in, up_copy, t, False)

        @pl.when(t < down)
        def _():
            relay(lax.rem(z + zs - down + t, zs), dn_out, dn_in, dn_copy, t, False)

        return carry

    lax.fori_loop(1, up, ring, 0)

    body, sq = pair_sum(z)
    up_copy(up - 1).wait_recv()
    dn_copy(down - 1).wait_recv()
    body = (
        body
        + up_in[up - 1, 0:half, :].astype(jnp.float32)
        + dn_in[down - 1, 0:half, :].astype(jnp.float32)
    )
    sq = (
        sq
        + join_rows(up_in[up - 1, half : half + 16, :])
        + join_rows(dn_in[down - 1, half : half + 16, :])
    )
    factor = lax.rsqrt(sq[0:1, :] / features + EPS)
    row = lax.broadcasted_iota(jnp.int32, (half, wide), 0) + c * half
    lane = lax.broadcasted_iota(jnp.int32, (half, wide), 1)
    factor = jnp.sum(jnp.where(row == lane, factor, 0.0), axis=1, keepdims=True)
    gate = body[:, 0:cols] * factor
    lift = body[:, cols : 2 * cols] * factor
    ibuf[2 * z + c] = (gate / (1.0 + jnp.exp(-gate)) * lift).astype(jnp.bfloat16)

    acc[...] = jnp.zeros_like(acc)

    def visit(zb):
        block = ibuf[pl.ds(2 * zb, 2)].reshape(cap, cols)
        acc[...] += rdot(block, wd_ref[pl.ds(pl.multiple_of(zb * cols, cols), cols), :])

    ring_gather(zs, ibuf, sems, lambda: visit(z), visit)

    produced = acc[...].astype(jnp.bfloat16)
    c_send[...] = rdot(unpack_ref[...], produced).astype(jnp.bfloat16).reshape(c_send.shape)
    swap_exp(peers, c_send, c_recv, cs_sem, cr_sem)
    back = c_recv[...].reshape(peers * SRC_CAP, width)
    out_ref[...] = (hid[:, 0:width] + rdot(mix_ref[...], back)).astype(jnp.bfloat16)

    def drain(d, carry):
        to_twin(d).wait_send()
        return carry

    lax.fori_loop(0, zs, drain, 0)

    def drain_ring(t, carry):
        up_copy(t).wait_send()

        @pl.when(t < down)
        def _():
            dn_copy(t).wait_send()

        return carry

    lax.fori_loop(0, up, drain_ring, 0)


def call(body, out, scratch, number, operands, spaces=None):
    spaces = spaces or [VMEM] * len(operands)
    return pl.pallas_call(
        body,
        out_shape=out,
        in_specs=[pl.BlockSpec(memory_space=space) for space in spaces],
        out_specs=pl.BlockSpec(memory_space=VMEM),
        scratch_shapes=scratch,
        compiler_params=pltpu.CompilerParams(
            collective_id=number, has_side_effects=True, vmem_limit_bytes=VMEM_BYTES
        ),
    )(*operands)


def tables(routes, route_weights, peers, cap):
    e = lax.axis_index("exp")
    tokens = routes.shape[0]
    block = tokens // peers
    experts = jnp.arange(peers, dtype=jnp.int32)
    slot = jnp.arange(SRC_CAP, dtype=jnp.int32)
    named = lax.dynamic_slice_in_dim(routes, e * block, block, 0)
    weights = lax.dynamic_slice_in_dim(route_weights, e * block, block, 0).astype(jnp.float32)
    hit = named[:, :, None] == experts[None, None, :]
    chosen = jnp.any(hit, axis=1)
    weight = jnp.sum(jnp.where(hit, weights[:, :, None], 0.0), axis=1)
    order = jnp.arange(block, dtype=jnp.int32)
    earlier = (order[None, :] < order[:, None]).astype(jnp.bfloat16)
    rank = rdot(earlier, chosen.astype(jnp.bfloat16)).astype(jnp.int32)
    rank = jnp.where(chosen, rank, -1)
    pick = (rank.T[:, None, :] == slot[None, :, None]).astype(jnp.bfloat16)
    pick = pick.reshape(peers * SRC_CAP, block)
    mix = jnp.where(rank[:, :, None] == slot[None, None, :], weight[:, :, None], 0.0)
    mix = mix.astype(jnp.bfloat16).reshape(block, peers * SRC_CAP)
    count = jnp.sum((routes == e).astype(jnp.int32).reshape(peers, -1), axis=1)
    start = jnp.sum(jnp.where(experts[None, :] < experts[:, None], count[None, :], 0), axis=1)
    at = jnp.where(slot[None, :] < count[:, None], start[:, None] + slot[None, :], -1)
    at = at.reshape(peers * SRC_CAP)
    rows = jnp.arange(cap, dtype=jnp.int32)
    pack = (rows[:, None] == at[None, :]).astype(jnp.bfloat16)
    unpack = (at[:, None] == rows[None, :]).astype(jnp.bfloat16)
    return pick, mix, pack, unpack


def local(
    zs,
    peers,
    queries,
    latents,
    cache,
    prefix_len,
    value_up,
    out_proj,
    residual,
    norm_gain,
    w_gate,
    w_up,
    w_down,
    routes,
    route_weights,
):
    bf16, f32 = jnp.bfloat16, jnp.float32
    dma = pltpu.SemaphoreType.DMA
    tok, heads, qwidth = queries.shape
    slots = cache.shape[0]
    width = residual.shape[1]
    block = residual.shape[0]
    inner = out_proj.shape[0]
    cap = SRC_CAP * min(peers, 6)
    half = cap // 2
    wide = -(-(width + 3) // 128) * 128
    eff = w_gate.shape[2]
    cols = eff // zs
    up, down = zs // 2, zs // 2 - 1
    features = width * 2 * zs
    rows = tok * heads

    pick, mix, pack, unpack = tables(routes, route_weights, peers, cap)
    q = jnp.swapaxes(queries, 0, 1).reshape(rows, qwidth)
    head_out = call(
        functools.partial(attention_kernel, zs),
        jax.ShapeDtypeStruct((tok, inner), bf16),
        [
            VMEM((2 * zs, tok + slots, qwidth), bf16),
            VMEM((rows, 1), f32),
            VMEM((rows, 1), f32),
            VMEM((rows, LAT), f32),
        ]
        + ring_sems(zs),
        1,
        (q, latents, cache, prefix_len, value_up),
        [VMEM, VMEM, VMEM, pltpu.SMEM, VMEM],
    )
    attended = call(
        functools.partial(project_kernel, zs, peers),
        jax.ShapeDtypeStruct((block, width), f32),
        [
            VMEM((2 * zs, tok, inner), bf16),
            VMEM((peers, block, width), bf16),
            VMEM((peers, block, width), bf16),
            dma((peers,)),
            dma((peers,)),
        ]
        + ring_sems(zs),
        2,
        (head_out, out_proj),
    )
    gain = jnp.pad(norm_gain, (0, wide - width)).reshape(1, wide)
    return call(
        functools.partial(experts_kernel, zs, peers, features),
        jax.ShapeDtypeStruct((block, width), bf16),
        [
            VMEM((block, wide), f32),
            VMEM((peers, SRC_CAP, wide), bf16),
            VMEM((peers, SRC_CAP, wide), bf16),
            VMEM((cap, wide), bf16),
            VMEM((16, 2 * cols), f32),
            VMEM((zs, half, 2 * cols), f32),
            VMEM((zs, half + 16, 2 * cols), bf16),
            VMEM((zs, half + 16, 2 * cols), bf16),
            VMEM((up, half + 16, 2 * cols), bf16),
            VMEM((up, half + 16, 2 * cols), bf16),
            VMEM((down, half + 16, 2 * cols), bf16),
            VMEM((down, half + 16, 2 * cols), bf16),
            VMEM((2 * zs, half, cols), bf16),
            VMEM((cap, width), f32),
            VMEM((peers, SRC_CAP, width), bf16),
            VMEM((peers, SRC_CAP, width), bf16),
            dma((peers,)),
            dma((peers,)),
            dma((zs,)),
            dma((zs,)),
            dma((up,)),
            dma((up,)),
            dma((down,)),
            dma((down,)),
            dma((peers,)),
            dma((peers,)),
        ]
        + ring_sems(zs),
        3,
        (
            attended,
            residual,
            gain,
            pick,
            mix,
            pack,
            unpack,
            w_gate[0],
            w_up[0],
            w_down[0],
        ),
    )


def solution(mesh):
    in_specs = (
        P("seq", "exp", None),
        P("seq", None),
        P("seq", None),
        P(),
        P("exp", None, None),
        P("exp", "seq"),
        P("exp", "seq"),
        P("seq"),
        P("exp", "seq", None),
        P("exp", "seq", None),
        P("exp", None, "seq"),
        P(),
        P(),
    )
    zs, peers = mesh.shape["seq"] // 2, mesh.shape["exp"]
    return jax.shard_map(
        functools.partial(local, zs, peers),
        mesh=mesh,
        in_specs=in_specs,
        out_specs=P("exp", "seq"),
        check_vma=False,
    )
```

time: 799 us -> 221 us (0.28)
  waiting for transfers between devices: 555 us -> 0 us
  Pallas kernels: 0 us -> 211 us
  blocking collectives: 131 us -> 0 us
  other arithmetic: 53.1 us -> 1.41 us
  matrix products: 24.4 us -> 0.16 us
  between operations: 15 us -> 0.89 us
  local copies, waits for them, and re-layouts: 18.9 us -> 7.55 us
    psum x2 -> x0, waiting for transfers between devices: 334 us -> none  [the longest x1 212 us: local(): up_full = lax.psum(up_part.astype(jnp.bfloat16), 'seq').astype(jnp.float32)]
    pallas_call x0 -> x3, Pallas kernels: none -> 211 us  [call(): pl.pallas_call(body, out_shape=out, in_specs=[pl.BlockSpec(memory_space=s...]
    all_gather x3 -> x0, waiting for transfers between devices: 133 us -> none  [the longest x1 75 us: local(): lax.all_gather(head_out, 'seq', axis=0, tiled=True)]
    psum x1 -> x0, blocking collectives: 90.6 us -> none  [local(): squares = lax.psum(jnp.sum(hidden_all * hidden_all, axis=1), 'seq')]
    reduce_scatter x1 -> x0, waiting for transfers between devices: 87.5 us -> none  [local(): lax.psum_scatter(placed.astype(jnp.bfloat16), 'exp', scatter_dimension=0,...]
    all_gather x1 -> x0, blocking collectives: 40.2 us -> none  [local(): piece = lax.all_gather(cache, 'seq', axis=0, tiled=True)]
    scatter-add x2 -> x0, other arithmetic: 32.7 us -> none  [the longest x1 28.8 us: local(): jnp.nonzero(chosen, size=held_cap, fill_value=0)[0].astype(jnp.int32)]
    dot_general x9 -> x1, matrix products: 24.4 us -> 0.16 us  [rdot(): return jnp.dot(a, b, preferred_element_type=jnp.float32)]
  transfers between devices with their start and end apart: 6 -> 0, of which waited for: 6 -> 0; matrix products, arithmetic and copies ran while one was open for 6% -> 0% of each run, Pallas kernels for 0% -> 0%
where the time goes in v1:
time: 221 us
  Pallas kernels  211 us (95%)
  local copies, waits for them, and re-layouts  7.55 us (3%)
    pallas_call x3, Pallas kernels, call(): pl.pallas_call(body, out_shape=out, in_specs=[pl.BlockSpec(memory_space=s...  211 us
    unnamed x24, local copies, waits for them, and re-layouts  4.98 us

profile of v1, /device:TPU:1, one launch (start us, length us, event | category | flops | bytes accessed | tf_op | source)
XLA Modules:
  0.0 220.7 jit_solution(13343995582902615947)
XLA Ops:
  0.0 0.7 constant_dynamic-slice_fusion
  0.7 0.7 dynamic-slice_convert_fusion
  1.4 0.1 copy.37
  1.6 0.2 fusion
  1.8 0.1 eq.102
  1.9 0.2 copy.36
  2.1 0.1 eq.99
  2.1 0.0 copy-start.6
  2.2 0.1 select_convert_fusion.mix_ref
  2.2 0.0 copy-start.4
  2.2 0.1 fusion.2.pick_ref
  2.4 0.7 copy-done.6
  3.1 0.1 reduce_sum.37
  3.2 0.1 select_reduce_fusion.1
  3.3 0.1 add.28
  3.4 0.1 add.29
  3.5 0.1 lt.55
  3.6 0.1 lt.56
  3.7 0.1 fusion.1.unpack_ref
  3.9 0.0 copy-done.4
  3.9 0.0 copy-start.7
  3.9 0.0 copy-start.2
  3.9 0.3 copy.33
  4.2 0.6 copy-done.7
  4.8 0.0 copy-start.3
  4.8 0.2 copy.34.lat_ref
  5.6 0.0 copy-done.2
  5.6 0.0 copy-done.3
  5.6 0.0 copy-start.5
  5.6 59.6 %shard_map.127.head_ref = bf16[128,512]{1,0:T(8,128)(2,1)S(1)} custom-call(bf16[512,576]{1,0:T(8,128)(2,1)S(1)} %bitcast.15, bf16[128,576]{1,0:T(8,128)(2,1)S(1)} %copy.34.lat_ref, bf16[16,576]{1,0:T(8,128)(2,1)S(1)} %copy-done.3, s32[1]{0:T(128)S(6)} %copy.41.live_ref, bf16[4,512,128]{2,1,0:T(8,128)(2,1)S(1)} %copy-done.2), custom_call_target="tpu_custom_call" | custom-call | tf_op jit(solution)/shard_map/pallas_call | solution.py:540
  65.3 0.0 copy-done.5
  65.3 0.1 copy.35.proj_ref
  65.4 68.7 %shard_map.128.att_ref = f32[256,224]{1,0:T(8,128)S(1)} custom-call(bf16[128,512]{1,0:T(8,128)(2,1)S(1)} %shard_map.127.head_ref, bf16[512,224]{1,0:T(8,128)(2,1)S(1)} %copy.35.proj_ref), custom_call_target="tpu_custom_call" | custom-call | tf_op jit(solution)/shard_map/pallas_call | solution.py:540
  134.2 0.0 copy-start.8
  134.2 0.0 copy-start
  134.2 1.5 copy.38
  135.7 0.0 copy-done.8
  135.7 0.0 copy-start.9
  135.8 0.1 copy.39.res_ref
  135.9 0.6 copy-done.9
  136.4 0.0 copy-done
  136.4 0.0 copy-start.1
  136.4 1.2 copy-done.1
  137.6 82.3 %shard_map.129 = bf16[256,224]{1,0:T(8,128)(2,1)S(1)} custom-call(f32[256,224]{1,0:T(8,128)S(1)} %shard_map.128.att_ref, bf16[256,224]{1,0:T(8,128)(2,1)S(1)} %copy.39.res_ref, f32[1,256]{1,0:T(1,128)S(1)} %bitcast.18, bf16[512,256]{1,0:T(8,128)(2,1)S(1)} %fusion.2.pick_ref, bf16[256,512]{1,0:T(8,128)(2,1)S(1)} %select_convert_fusion.mix_ref, ...), custom_call_target="tpu_custom_call" | custom-call | tf_op jit(solution)/shard_map/pallas_call | solution.py:540
  219.9 0.8 copy.40
  (9 shorter events, 0.2 us)
Async XLA Ops:
  2.1 0.9 copy-start.6
  2.2 1.6 copy-start.4
  3.9 0.9 copy-start.7
  3.9 1.7 copy-start.2
  4.8 0.8 copy-start.3
  5.6 59.6 %copy-start.5 = (bf16[512,224]{0,1:T(8,128)(2,1)S(1)}, bf16[512,224]{0,1:T(8,128)(2,1)}, u32[]{:S(2)}) copy-start(bf16[512,224]{0,1:T(8,128)(2,1)} %param.18) | copy-start | bytes 688132
  134.2 1.6 copy-start.8
  134.2 2.3 %copy-start = (bf16[1,224,2048]{2,1,0:T(8,128)(2,1)S(1)}, bf16[1,224,2048]{2,1,0:T(8,128)(2,1)}, u32[]{:S(2)}) copy-start(bf16[1,224,2048]{2,1,0:T(8,128)(2,1)} %param.21) | copy-start | bytes 2752516
  135.7 0.7 copy-start.9
  136.4 1.2 copy-start.1

commit v2 on v1

--- a/solution.py
+++ b/solution.py
@@ -1,4 +1,5 @@
 import functools
+import math
 
 import jax
 import jax.numpy as jnp
@@ -39,136 +40,198 @@
     return z, c, above, below, twin
 
 
-def greet(zs, peers):
-    _, _, above, below, twin = place(zs)
+def greet(zs, reach, peers):
+    z, c, _, _, twin = place(zs)
+    s = 2 * z + c
     e = lax.axis_index("exp")
     barrier = pltpu.get_barrier_semaphore()
-    for to in (above, below, twin):
+
+    def hello(seq, exp):
         pl.semaphore_signal(
-            barrier, inc=1, device_id={"seq": to, "exp": e}, device_id_type=MESH
+            barrier, inc=1, device_id={"seq": seq, "exp": exp}, device_id_type=MESH
         )
-    if peers > 1:
-        s = lax.axis_index("seq")
-
-        def hello(j, carry):
-            pl.semaphore_signal(
-                barrier,
-                inc=1,
-                device_id={"seq": s, "exp": lax.rem(e + j, peers)},
-                device_id_type=MESH,
-            )
-            return carry
-
-        lax.fori_loop(1, peers, hello, 0)
-    pl.semaphore_wait(barrier, 3 + max(peers - 1, 0))
-
-
-def ring_sems(zs):
+
+    hello(twin, e)
+    for k in range(1, reach + 1):
+        hello(lax.rem(z + k, zs) * 2 + c, e)
+        hello(lax.rem(z + zs - k, zs) * 2 + c, e)
+
+    def along(j, carry):
+        hello(s, lax.rem(e + j, peers))
+        return carry
+
+    lax.fori_loop(1, peers, along, 0)
+    pl.semaphore_wait(barrier, 1 + 2 * reach + peers - 1)
+
+
+def remote(src, dst, ssem, rsem, seq, exp):
+    return pltpu.make_async_remote_copy(
+        src_ref=src,
+        dst_ref=dst,
+        send_sem=ssem,
+        recv_sem=rsem,
+        device_id={"seq": seq, "exp": exp},
+        device_id_type=MESH,
+    )
+
+
+def ring_sems(zs, parts):
+    dma = pltpu.SemaphoreType.DMA
+    return [dma((zs, parts)), dma((zs, parts)), dma((zs,)), dma((zs,))]
+
+
+def ring_gather(zs, buf, sems, own, visit, stride=1, parts=1, after=None, delay=0):
+    rs, rr, ts, tr = sems
     up, down = zs // 2, zs // 2 - 1
-    dma = pltpu.SemaphoreType.DMA
-    return [dma((up,)), dma((up,)), dma((down,)), dma((down,)), dma((zs,)), dma((zs,))]
-
-
-def ring_gather(zs, buf, sems, own, visit):
-    us, ur, ds, dr, ts, tr = sems
-    up, down = zs // 2, zs // 2 - 1
-    z, c, above, below, twin = place(zs)
+    z, c, _, _, twin = place(zs)
     e = lax.axis_index("exp")
-
-    def copy(zb, core, ssem, rsem, to):
+    size = buf.shape[1] // parts
+
+    def far(side, k):
+        return lax.rem(z + (zs - k if side == 0 else k), zs)
+
+    def index(side, k):
+        return k if side == 0 else up + k
+
+    def hop(side, k, p, step):
+        slot = buf.at[2 * far(side, k) + c, pl.ds(p * size, size)]
+        i = index(side, k + step)
+        to = lax.rem(z + (step if side == 0 else zs - step), zs) * 2 + c
+        return remote(slot, slot, rs.at[i, p], rr.at[i, p], to, e)
+
+    def came(side, k, p):
+        slot = buf.at[2 * far(side, k) + c, pl.ds(p * size, size)]
+        i = index(side, k)
+        return remote(slot, slot, rs.at[i, p], rr.at[i, p], twin, e)
+
+    def share(i, zb, core):
         slot = buf.at[2 * zb + core]
-        return pltpu.make_async_remote_copy(
-            src_ref=slot,
-            dst_ref=slot,
-            send_sem=ssem,
-            recv_sem=rsem,
-            device_id={"seq": to, "exp": e},
-            device_id_type=MESH,
-        )
-
-    def lower(k):
-        return lax.rem(z - k + zs, zs)
-
-    def upper(k):
-        return lax.rem(z + k, zs)
-
-    copy(z, c, us.at[0], ur.at[0], above).start()
-    copy(z, c, ds.at[0], dr.at[0], below).start()
-    copy(z, c, ts.at[0], tr.at[0], twin).start()
+        return remote(slot, slot, ts.at[i], tr.at[i], twin, e)
+
+    limits = (up, down)
+    for p in range(parts):
+        for k in range(1, stride + 1):
+            for side in range(2):
+                if k <= limits[side]:
+                    hop(side, 0, p, k).start()
+    share(0, z, c).start()
 
     def step(k, carry):
-        @pl.when(k <= up)
-        def _():
-            copy(lower(k), c, us.at[k - 1], ur.at[k - 1], above).wait_recv()
-
-            @pl.when(k < up)
+        for side in range(2):
+
+            @pl.when(k <= limits[side])
             def _():
-                copy(lower(k), c, us.at[k], ur.at[k], above).start()
-
-            copy(lower(k), c, ts.at[k], tr.at[k], twin).start()
-
-        @pl.when(k <= down)
-        def _():
-            copy(upper(k), c, ds.at[k - 1], dr.at[k - 1], below).wait_recv()
-
-            @pl.when(k < down)
-            def _():
-                copy(upper(k), c, ds.at[k], dr.at[k], below).start()
-
-            copy(upper(k), c, ts.at[up + k], tr.at[up + k], twin).start()
+                for p in range(parts):
+                    came(side, k, p).wait_recv()
+
+                    @pl.when(k + stride <= limits[side])
+                    def _():
+                        hop(side, k, p, stride).start()
+
+                share(index(side, k), far(side, k), c).start()
 
         @pl.when(k == 1)
         def _():
-            copy(z, 1 - c, ts.at[0], tr.at[0], twin).wait_recv()
+            share(0, z, 1 - c).wait_recv()
             own()
 
-        def side(which, inner):
-            j = k - 1
-
-            @pl.when((which == 0) | (j <= down))
+        def both(j, act):
+            def one(side, inner):
+                @pl.when((side == 0) | (j <= down))
+                def _():
+                    zb = lax.rem(z + jnp.where(side == 0, zs - j, j), zs)
+                    act(zb, jnp.where(side == 0, j, up + j))
+
+                return inner
+
+            lax.fori_loop(0, 2, one, 0)
+
+        def arrive(zb, i):
+            share(i, zb, 1 - c).wait_recv()
+            visit(zb)
+
+        @pl.when((k > 1) & (k <= up + 1))
+        def _():
+            both(k - 1, arrive)
+
+        if after is not None:
+
+            @pl.when(k == delay + 1)
             def _():
-                zb = lax.rem(z + jnp.where(which == 0, zs - j, j), zs)
-                index = jnp.where(which == 0, j, up + j)
-                copy(zb, 1 - c, ts.at[index], tr.at[index], twin).wait_recv()
-                visit(zb)
-
-            return inner
-
-        @pl.when(k > 1)
-        def _():
-            lax.fori_loop(0, 2, side, 0)
-
-        return carry
-
-    lax.fori_loop(1, up + 2, step, 0)
+                after(z)
+
+            @pl.when(k > delay + 1)
+            def _():
+                both(k - 1 - delay, lambda zb, i: after(zb))
+
+        return carry
+
+    lax.fori_loop(1, up + 2 + delay, step, 0)
 
     def drain(k, carry):
-        copy(lower(k), c, us.at[k], ur.at[k], above).wait_send()
-        copy(lower(k), c, ts.at[k], tr.at[k], twin).wait_send()
-
-        @pl.when(k < down)
-        def _():
-            copy(upper(k), c, ds.at[k], dr.at[k], below).wait_send()
-            copy(upper(k), c, ts.at[up + 1 + k], tr.at[up + 1 + k], twin).wait_send()
-
-        return carry
-
-    lax.fori_loop(0, up, drain, 0)
-    copy(lower(up), c, ts.at[up], tr.at[up], twin).wait_send()
+        for side in range(2):
+
+            @pl.when(k <= limits[side])
+            def _():
+                for p in range(parts):
+                    came(side, k, p).wait_send()
+                share(index(side, k), far(side, k), c).wait_send()
+
+        return carry
+
+    lax.fori_loop(1, up + 1, drain, 0)
+    share(0, z, c).wait_send()
 
 
 def attention_kernel(
-    zs, q_ref, lat_ref, cache_ref, live_ref, vup_ref, out_ref, buf, best, total, acc, *sems
+    zs,
+    peers,
+    side,
+    q_ref,
+    lat_ref,
+    cache_ref,
+    live_ref,
+    vup_ref,
+    out_ref,
+    buf,
+    cbuf,
+    best,
+    total,
+    acc,
+    rs,
+    rr,
+    cs,
+    cr,
+    ls,
+    lr,
+    ms,
+    mr,
+    ts,
+    tr,
+    ns,
+    nr,
 ):
     tok = lat_ref.shape[0]
     slots = cache_ref.shape[0]
     rows, width = q_ref.shape
     heads = rows // tok
-    z, c, _, _, _ = place(zs)
+    stride = 2
+    up, down = zs // 2, zs // 2 - 1
+    limits = (up, down)
+    z, c, _, _, twin = place(zs)
     s = 2 * z + c
-    greet(zs, 0)
-    buf[s, 0:tok, :] = lat_ref[...]
-    buf[s, tok : tok + slots, :] = cache_ref[...]
+    e = lax.axis_index("exp")
+    ey, ex = e // side, lax.rem(e, side)
+    q = jnp.where(c == 0, ex, ey)
+    size = tok // side
+
+    def line(j):
+        p = lax.rem(q + j, side)
+        return jnp.where(c == 0, ey * side + p, p * side + ex)
+
+    greet(zs, stride, peers)
+    buf[s] = lat_ref[...]
+    cbuf[s] = cache_ref[...]
 
     def absorb(keys, visible, first):
         scores = rdot_t(q_ref[...], keys) * SCALE
@@ -190,25 +253,156 @@
         best[...] = newest
 
     def pair(zb):
-        return buf[pl.ds(2 * zb, 2), 0:tok, :].reshape(2 * tok, width)
-
-    def own():
-        row = lax.broadcasted_iota(jnp.int32, (rows, 2 * tok), 0)
-        key = lax.broadcasted_iota(jnp.int32, (rows, 2 * tok), 1)
-        absorb(pair(z), key <= lax.rem(row, tok) + c * tok, True)
-
-    def visit(zb):
-        @pl.when(zb < z)
+        return buf[pl.ds(2 * zb, 2)].reshape(2 * tok, width)
+
+    def far(way, k):
+        return lax.rem(z + (zs - k if way == 0 else k), zs)
+
+    def index(way, k):
+        return k if way == 0 else up + k
+
+    def piece(zb, p):
+        return buf.at[2 * zb + c, pl.ds(pl.multiple_of(p * size, size), size)]
+
+    def hop(way, k, step):
+        i = index(way, k + step)
+        to = lax.rem(z + (step if way == 0 else zs - step), zs) * 2 + c
+        slot = piece(far(way, k), q)
+        return remote(slot, slot, rs.at[i], rr.at[i], to, e)
+
+    def cache_hop(way, k, step):
+        i = index(way, k + step)
+        to = lax.rem(z + (step if way == 0 else zs - step), zs) * 2 + c
+        slot = cbuf.at[2 * far(way, k) + c]
+        return remote(slot, slot, cs.at[i], cr.at[i], to, e)
+
+    def came(way, k):
+        i = index(way, k)
+        slot = piece(far(way, k), q)
+        return remote(slot, slot, rs.at[i], rr.at[i], twin, e)
+
+    def cache_came(way, k):
+        i = index(way, k)
+        slot = cbuf.at[2 * far(way, k) + c]
+        return remote(slot, slot, cs.at[i], cr.at[i], twin, e)
+
+    def spread(i, zb, j):
+        slot = piece(zb, q)
+        return remote(slot, slot, ls.at[i, j], lr.at[i, j], s, line(j))
+
+    def spread_in(i, zb, j):
+        slot = piece(zb, lax.rem(q + side - j, side))
+        return remote(slot, slot, ls.at[i, j], lr.at[i, j], s, line(j))
+
+    def cache_spread(i, zb, j):
+        slot = cbuf.at[2 * zb + c]
+        return remote(slot, slot, ms.at[i, j], mr.at[i], s, line(j))
+
+    def share(i, zb, core):
+        slot = buf.at[2 * zb + core]
+        return remote(slot, slot, ts.at[i], tr.at[i], twin, e)
+
+    def cache_share(i, zb, core):
+        slot = cbuf.at[2 * zb + core]
+        return remote(slot, slot, ns.at[i], nr.at[i], twin, e)
+
+    def carries(zb):
+        return lax.rem(zb, side) == q
+
+    for k in range(1, stride + 1):
+        for way in range(2):
+            if k <= limits[way]:
+                hop(way, 0, k).start()
+
+                @pl.when(carries(z))
+                def _():
+                    cache_hop(way, 0, k).start()
+
+    share(0, z, c).start()
+    cache_share(0, z, c).start()
+
+    def step(k, carry):
+        for way in range(2):
+            zb, i = far(way, k), index(way, k)
+
+            @pl.when(k <= limits[way])
+            def _():
+                came(way, k).wait_recv()
+
+                @pl.when(k + stride <= limits[way])
+                def _():
+                    hop(way, k, stride).start()
+
+                @pl.when(zb < z)
+                def _():
+                    for j in range(1, side):
+                        spread(i, zb, j).start()
+
+                @pl.when(carries(zb))
+                def _():
+                    cache_came(way, k).wait_recv()
+
+                    @pl.when(k + stride <= limits[way])
+                    def _():
+                        cache_hop(way, k, stride).start()
+
+                    for j in range(1, side):
+                        cache_spread(i, zb, j).start()
+
+        for way in range(2):
+            zl, il = far(way, k - 1), index(way, k - 1)
+
+            @pl.when((k > 1) & (k - 1 <= limits[way]))
+            def _():
+                @pl.when(zl < z)
+                def _():
+                    for j in range(1, side):
+                        spread_in(il, zl, j).wait_recv()
+                    share(il, zl, c).start()
+
+                @pl.when(jnp.logical_not(carries(zl)))
+                def _():
+                    cache_spread(il, zl, 1).wait_recv()
+
+                cache_share(il, zl, c).start()
+
+        @pl.when(k == 2)
         def _():
-            absorb(pair(zb), None, False)
-
-    ring_gather(zs, buf, sems, own, visit)
+            share(0, z, 1 - c).wait_recv()
+            cache_share(0, z, 1 - c).wait_recv()
+            row = lax.broadcasted_iota(jnp.int32, (rows, 2 * tok), 0)
+            key = lax.broadcasted_iota(jnp.int32, (rows, 2 * tok), 1)
+            absorb(pair(z), key <= lax.rem(row, tok) + c * tok, True)
+
+        def one(way, inner):
+            j = k - 2
+
+            @pl.when((way == 0) | (j <= down))
+            def _():
+                zb = lax.rem(z + jnp.where(way == 0, zs - j, j), zs)
+                i = jnp.where(way == 0, j, up + j)
+                cache_share(i, zb, 1 - c).wait_recv()
+
+                @pl.when(zb < z)
+                def _():
+                    share(i, zb, 1 - c).wait_recv()
+                    absorb(pair(zb), None, False)
+
+            return inner
+
+        @pl.when(k > 2)
+        def _():
+            lax.fori_loop(0, 2, one, 0)
+
+        return carry
+
+    lax.fori_loop(1, up + 3, step, 0)
 
     live = live_ref[0]
     group = max(1, min(256, slots * 2 * zs) // slots)
 
     def prefix(i, carry):
-        keys = buf[pl.ds(i * group, group), tok : tok + slots, :].reshape(group * slots, width)
+        keys = cbuf[pl.ds(i * group, group)].reshape(group * slots, width)
         key = lax.broadcasted_iota(jnp.int32, (rows, group * slots), 1) + i * (group * slots)
         absorb(keys, key < live, False)
         return carry
@@ -221,57 +415,130 @@
         vh = vup_ref.shape[2]
         out_ref[:, h * vh : (h + 1) * vh] = rdot(context, vup_ref[h]).astype(jnp.bfloat16)
 
-
-def project_kernel(zs, peers, head_ref, proj_ref, out_ref, buf, terms, got, t_send, t_recv, *sems):
+    def drain(k, carry):
+        for way in range(2):
+            zb, i = far(way, k), index(way, k)
+
+            @pl.when(k <= limits[way])
+            def _():
+                came(way, k).wait_send()
+
+                @pl.when(zb < z)
+                def _():
+                    for j in range(1, side):
+                        spread(i, zb, j).wait_send()
+                    share(i, zb, c).wait_send()
+
+                origin = jnp.maximum(k - stride, 0)
+
+                @pl.when(carries(lax.rem(z + (zs - origin if way == 0 else origin), zs)))
+                def _():
+                    cache_came(way, k).wait_send()
+
+                @pl.when(carries(zb))
+                def _():
+                    for j in range(1, side):
+                        cache_spread(i, zb, j).wait_send()
+
+                cache_share(i, zb, c).wait_send()
+
+        return carry
+
+    lax.fori_loop(1, up + 1, drain, 0)
+    share(0, z, c).wait_send()
+    cache_share(0, z, c).wait_send()
+
+
+def project_kernel(
+    zs,
+    peers,
+    side,
+    head_ref,
+    proj_ref,
+    out_ref,
+    buf,
+    terms,
+    row_in,
+    sums,
+    col_in,
+    x_send,
+    x_recv,
+    y_send,
+    y_recv,
+    *sems,
+):
     tok, inner = head_ref.shape
-    width = proj_ref.shape[1]
     z, c, _, _, _ = place(zs)
     s = 2 * z + c
     e = lax.axis_index("exp")
-    greet(zs, peers)
+    ey, ex = e // side, lax.rem(e, side)
+    greet(zs, 1, peers)
     buf[s] = head_ref[...]
 
-    def hand(zb):
-        return pltpu.make_async_remote_copy(
-            src_ref=terms.at[zb],
-            dst_ref=got.at[e],
-            send_sem=t_send.at[zb],
-            recv_sem=t_recv.at[e],
-            device_id={"seq": s, "exp": zb},
-            device_id_type=MESH,
+    def along_x(zb):
+        to_y, to_x = zb // side, lax.rem(zb, side)
+        return remote(
+            terms.at[zb],
+            row_in.at[to_y, ex],
+            x_send.at[zb],
+            x_recv.at[to_y, ex],
+            s,
+            ey * side + to_x,
+        )
+
+    def along_y(to_y):
+        return remote(
+            sums.at[to_y], col_in.at[ey], y_send.at[to_y], y_recv.at[ey], s, to_y * side + ex
         )
 
     def visit(zb):
         rows = buf[pl.ds(2 * zb, 2)].reshape(2 * tok, inner)
         terms[zb] = rdot(rows, proj_ref[...]).astype(jnp.bfloat16)
 
-        @pl.when(zb != e)
+        @pl.when(lax.rem(zb, side) != ex)
         def _():
-            hand(zb).start()
-
-    ring_gather(zs, buf, sems, lambda: visit(z), visit)
-    out_ref[...] = terms[e].astype(jnp.float32)
-
-    def collect(j, carry):
-        g = lax.rem(e + j, peers)
-        pltpu.make_async_remote_copy(
-            src_ref=terms.at[g],
-            dst_ref=got.at[g],
-            send_sem=t_send.at[g],
-            recv_sem=t_recv.at[g],
-            device_id={"seq": s, "exp": g},
-            device_id_type=MESH,
-        ).wait_recv()
-        out_ref[...] += got[g].astype(jnp.float32)
-        return carry
-
-    lax.fori_loop(1, peers, collect, 0)
-
-    def drain(j, carry):
-        hand(lax.rem(e + j, peers)).wait_send()
-        return carry
-
-    lax.fori_loop(1, peers, drain, 0)
+            along_x(zb).start()
+
+    def after(zb):
+        @pl.when(lax.rem(zb, side) == ex)
+        def _():
+            to_y = zb // side
+            part = terms[zb].astype(jnp.float32)
+            for j in range(1, side):
+                g = lax.rem(ex + j, side)
+                slot = row_in.at[to_y, g]
+                remote(
+                    slot, slot, x_send.at[zb], x_recv.at[to_y, g], s, ey * side + g
+                ).wait_recv()
+                part = part + row_in[to_y, g].astype(jnp.float32)
+
+            @pl.when(to_y == ey)
+            def _():
+                out_ref[...] = part
+
+            @pl.when(to_y != ey)
+            def _():
+                sums[to_y] = part.astype(jnp.bfloat16)
+                along_y(to_y).start()
+
+    ring_gather(zs, buf, sems, lambda: visit(z), visit, parts=2, after=after, delay=2)
+
+    for j in range(1, side):
+        g = lax.rem(ey + j, side)
+        slot = col_in.at[g]
+        remote(slot, slot, y_send.at[g], y_recv.at[g], s, g * side + ex).wait_recv()
+        out_ref[...] += col_in[g].astype(jnp.float32)
+
+    def drain(zb, carry):
+        @pl.when(lax.rem(zb, side) != ex)
+        def _():
+            along_x(zb).wait_send()
+
+        return carry
+
+    lax.fori_loop(0, zs, drain, 0)
+    for j in range(1, side):
+        along_y(lax.rem(ey + j, side)).wait_send()
 
 
 def swap_exp(peers, send, recv, s_sem, r_sem):
@@ -337,10 +604,12 @@
     wu_ref,
     wd_ref,
     out_ref,
+    wgu,
     hid,
     d_send,
     d_recv,
     xs,
+    xo,
     sqv,
     mine,
     other,
@@ -353,6 +622,7 @@
     acc,
     c_send,
     c_recv,
+    w_sem,
     ds_sem,
     dr_sem,
     ps_sem,
@@ -373,7 +643,24 @@
     up, down = zs // 2, zs // 2 - 1
     z, c, above, below, twin = place(zs)
     e = lax.axis_index("exp")
-    greet(zs, peers)
+
+    def load(d, which):
+        span = pl.ds(pl.multiple_of(d * cols, cols), cols)
+        return pltpu.make_async_copy(
+            (wg_ref, wu_ref)[which].at[:, span],
+            wgu.at[d, :, pl.ds(which * cols, cols)],
+            w_sem.at[d, which],
+        )
+
+    def load_all(i, carry):
+        t = i // 2
+        d = lax.rem(z + jnp.where(lax.rem(i, 2) == 0, up - t, zs - down + t), zs)
+        load(d, 0).start()
+        load(d, 1).start()
+        return carry
+
+    lax.fori_loop(0, zs, load_all, 0)
+    greet(zs, 2, peers)
 
     hid[...] = jnp.zeros_like(hid)
     hid[:, 0:width] = res_ref[...].astype(jnp.float32) + att_ref[...]
@@ -405,8 +692,8 @@
     sqv[:, 0:cap] = rdot_t(ones, packed)
     own_sq = sqv[...]
     tail = split_rows(own_sq)
-    x_mine = xs[pl.ds(pl.multiple_of(c * half, 16), half), 0:width]
-    x_other = xs[pl.ds(pl.multiple_of((1 - c) * half, 16), half), 0:width]
+    xo[0:half, :] = xs[pl.ds(pl.multiple_of(c * half, 16), half), 0:width]
+    xo[half:cap, :] = xs[pl.ds(pl.multiple_of((1 - c) * half, 16), half), 0:width]
 
     def to_twin(d):
         return pltpu.make_async_remote_copy(
@@ -418,19 +705,14 @@
             device_id_type=MESH,
         )
 
-    def partial(i, carry):
-        t = i // 2
-        d = lax.rem(z + jnp.where(lax.rem(i, 2) == 0, up - t, zs - down + t), zs)
-        span = pl.ds(pl.multiple_of(d * cols, cols), cols)
-        other[d, 0:half, 0:cols] = rdot(x_other, wg_ref[:, span]).astype(jnp.bfloat16)
-        other[d, 0:half, cols : 2 * cols] = rdot(x_other, wu_ref[:, span]).astype(jnp.bfloat16)
+    def partial(d):
+        load(d, 0).wait()
+        load(d, 1).wait()
+        both = rdot(xo[...], wgu[d])
+        other[d, 0:half, :] = both[half:].astype(jnp.bfloat16)
         other[d, half : half + 16, :] = tail
         to_twin(d).start()
-        mine[d, :, 0:cols] = rdot(x_mine, wg_ref[:, span])
-        mine[d, :, cols : 2 * cols] = rdot(x_mine, wu_ref[:, span])
-        return carry
-
-    lax.fori_loop(0, zs, partial, 0)
+        mine[d] = both[:half]
 
     def up_copy(t):
         return pltpu.make_async_remote_copy(
@@ -468,15 +750,30 @@
         out[t, half : half + 16, :] = split_rows(sq)
         copy(t).start()
 
-    relay(lax.rem(z + up, zs), up_out, up_in, up_copy, 0, True)
-    relay(lax.rem(z + zs - down, zs), dn_out, dn_in, dn_copy, 0, True)
+    def up_dest(t):
+        return lax.rem(z + up - t, zs)
+
+    def dn_dest(t):
+        return lax.rem(z + zs - down + t, zs)
+
+    partial(up_dest(0))
+    partial(dn_dest(0))
+    partial(up_dest(1))
+    partial(dn_dest(1))
+    relay(up_dest(0), up_out, up_in, up_copy, 0, True)
+    relay(dn_dest(0), dn_out, dn_in, dn_copy, 0, True)
 
     def ring(t, carry):
-        relay(lax.rem(z + up - t, zs), up_out, up_in, up_copy, t, False)
+        @pl.when(t < up - 1)
+        def _():
+            partial(up_dest(t + 1))
+            partial(dn_dest(t + 1))
+
+        relay(up_dest(t), up_out, up_in, up_copy, t, False)
 
         @pl.when(t < down)
         def _():
-            relay(lax.rem(z + zs - down + t, zs), dn_out, dn_in, dn_copy, t, False)
+            relay(dn_dest(t), dn_out, dn_in, dn_copy, t, False)
 
         return carry
 
@@ -509,7 +806,7 @@
         block = ibuf[pl.ds(2 * zb, 2)].reshape(cap, cols)
         acc[...] += rdot(block, wd_ref[pl.ds(pl.multiple_of(zb * cols, cols), cols), :])
 
-    ring_gather(zs, ibuf, sems, lambda: visit(z), visit)
+    ring_gather(zs, ibuf, sems, lambda: visit(z), visit, stride=2)
 
     produced = acc[...].astype(jnp.bfloat16)
     c_send[...] = rdot(unpack_ref[...], produced).astype(jnp.bfloat16).reshape(c_send.shape)
@@ -611,33 +908,51 @@
     features = width * 2 * zs
     rows = tok * heads
 
+    side = math.isqrt(peers)
+
     pick, mix, pack, unpack = tables(routes, route_weights, peers, cap)
     q = jnp.swapaxes(queries, 0, 1).reshape(rows, qwidth)
     head_out = call(
-        functools.partial(attention_kernel, zs),
+        functools.partial(attention_kernel, zs, peers, side),
         jax.ShapeDtypeStruct((tok, inner), bf16),
         [
-            VMEM((2 * zs, tok + slots, qwidth), bf16),
+            VMEM((2 * zs, tok, qwidth), bf16),
+            VMEM((2 * zs, slots, qwidth), bf16),
             VMEM((rows, 1), f32),
             VMEM((rows, 1), f32),
             VMEM((rows, LAT), f32),
-        ]
-        + ring_sems(zs),
+            dma((zs,)),
+            dma((zs,)),
+            dma((zs,)),
+            dma((zs,)),
+            dma((zs, side)),
+            dma((zs, side)),
+            dma((zs, side)),
+            dma((zs,)),
+            dma((zs,)),
+            dma((zs,)),
+            dma((zs,)),
+            dma((zs,)),
+        ],
         1,
         (q, latents, cache, prefix_len, value_up),
         [VMEM, VMEM, VMEM, pltpu.SMEM, VMEM],
     )
     attended = call(
-        functools.partial(project_kernel, zs, peers),
+        functools.partial(project_kernel, zs, peers, side),
         jax.ShapeDtypeStruct((block, width), f32),
         [
             VMEM((2 * zs, tok, inner), bf16),
             VMEM((peers, block, width), bf16),
-            VMEM((peers, block, width), bf16),
+            VMEM((side, side, block, width), bf16),
+            VMEM((side, block, width), bf16),
+            VMEM((side, block, width), bf16),
             dma((peers,)),
-            dma((peers,)),
+            dma((side, side)),
+            dma((side,)),
+            dma((side,)),
         ]
-        + ring_sems(zs),
+        + ring_sems(zs, 2),
         2,
         (head_out, out_proj),
     )
@@ -646,10 +961,12 @@
         functools.partial(experts_kernel, zs, peers, features),
         jax.ShapeDtypeStruct((block, width), bf16),
         [
+            VMEM((zs, width, 2 * cols), bf16),
             VMEM((block, wide), f32),
             VMEM((peers, SRC_CAP, wide), bf16),
             VMEM((peers, SRC_CAP, wide), bf16),
             VMEM((cap, wide), bf16),
+            VMEM((cap, width), bf16),
             VMEM((16, 2 * cols), f32),
             VMEM((zs, half, 2 * cols), f32),
             VMEM((zs, half + 16, 2 * cols), bf16),
@@ -662,6 +979,7 @@
             VMEM((cap, width), f32),
             VMEM((peers, SRC_CAP, width), bf16),
             VMEM((peers, SRC_CAP, width), bf16),
+            dma((zs, 2)),
             dma((peers,)),
             dma((peers,)),
             dma((zs,)),
@@ -673,7 +991,7 @@
             dma((peers,)),
             dma((peers,)),
         ]
-        + ring_sems(zs),
+        + ring_sems(zs, 1),
         3,
         (
             attended,
@@ -687,6 +1005,7 @@
             w_up[0],
             w_down[0],
         ),
+        [VMEM] * 7 + [pl.ANY, pl.ANY, VMEM],
     )
 
 

time: 221 us -> 187 us (0.85)
  Pallas kernels: 211 us -> 177 us
    pallas_call x3, Pallas kernels: 211 us -> 177 us  [call(): pl.pallas_call(body, out_shape=out, in_specs=[pl.BlockSpec(memory_space=s...]
where the time goes in v2:
time: 187 us
  Pallas kernels  177 us (95%)
  local copies, waits for them, and re-layouts  7.55 us (4%)
    pallas_call x3, Pallas kernels, call(): pl.pallas_call(body, out_shape=out, in_specs=[pl.BlockSpec(memory_space=s...  177 us
    unnamed x24, local copies, waits for them, and re-layouts  4.98 us

profile of v2, /device:TPU:1, one launch (start us, length us, event | category | flops | bytes accessed | tf_op | source)
XLA Modules:
  0.0 186.6 jit_solution(8604816850819294052)
XLA Ops:
  0.0 0.7 constant_dynamic-slice_fusion
  0.7 0.7 dynamic-slice_convert_fusion
  1.4 0.1 copy.37
  1.6 0.2 fusion
  1.8 0.1 eq.102
  1.9 0.2 copy.36
  2.1 0.1 eq.99
  2.1 0.0 copy-start.6
  2.2 0.1 select_convert_fusion.mix_ref
  2.2 0.0 copy-start.4
  2.2 0.1 fusion.2.pick_ref
  2.4 0.7 copy-done.6
  3.1 0.1 reduce_sum.37
  3.2 0.1 select_reduce_fusion.1
  3.3 0.1 add.28
  3.4 0.1 add.29
  3.5 0.1 lt.55
  3.6 0.1 lt.56
  3.7 0.1 fusion.1.unpack_ref
  3.9 0.0 copy-done.4
  3.9 0.0 copy-start.7
  3.9 0.0 copy-start.2
  3.9 0.3 copy.33
  4.2 0.6 copy-done.7
  4.8 0.0 copy-start.3
  4.8 0.2 copy.34.lat_ref
  5.6 0.0 copy-done.2
  5.6 0.0 copy-done.3
  5.6 0.0 copy-start.5
  5.6 47.5 %shard_map.127.head_ref = bf16[128,512]{1,0:T(8,128)(2,1)S(1)} custom-call(bf16[512,576]{1,0:T(8,128)(2,1)S(1)} %bitcast.15, bf16[128,576]{1,0:T(8,128)(2,1)S(1)} %copy.34.lat_ref, bf16[16,576]{1,0:T(8,128)(2,1)S(1)} %copy-done.3, s32[1]{0:T(128)S(6)} %copy.41.live_ref, bf16[4,512,128]{2,1,0:T(8,128)(2,1)S(1)} %copy-done.2), custom_call_target="tpu_custom_call" | custom-call | tf_op jit(solution)/shard_map/pallas_call | solution.py:837
  53.1 0.0 copy-done.5
  53.1 0.1 copy.35.proj_ref
  53.3 57.2 %shard_map.128.att_ref = f32[256,224]{1,0:T(8,128)S(1)} custom-call(bf16[128,512]{1,0:T(8,128)(2,1)S(1)} %shard_map.127.head_ref, bf16[512,224]{1,0:T(8,128)(2,1)S(1)} %copy.35.proj_ref), custom_call_target="tpu_custom_call" | custom-call | tf_op jit(solution)/shard_map/pallas_call | solution.py:837
  110.5 0.0 copy-start.8
  110.5 0.0 copy-start
  110.5 1.5 copy.38
  112.0 0.0 copy-done.8
  112.0 0.0 copy-start.9
  112.1 0.1 copy.39.res_ref
  112.2 0.6 copy-done.9
  112.7 0.0 copy-done
  112.7 0.0 copy-start.1
  112.7 1.2 copy-done.1
  113.9 71.9 %shard_map.129 = bf16[256,224]{1,0:T(8,128)(2,1)S(1)} custom-call(f32[256,224]{1,0:T(8,128)S(1)} %shard_map.128.att_ref, bf16[256,224]{1,0:T(8,128)(2,1)S(1)} %copy.39.res_ref, f32[1,256]{1,0:T(1,128)S(1)} %bitcast.18, bf16[512,256]{1,0:T(8,128)(2,1)S(1)} %fusion.2.pick_ref, bf16[256,512]{1,0:T(8,128)(2,1)S(1)} %select_convert_fusion.mix_ref, ...), custom_call_target="tpu_custom_call" | custom-call | tf_op jit(solution)/shard_map/pallas_call | solution.py:837
  185.8 0.8 copy.40
  (9 shorter events, 0.2 us)
Async XLA Ops:
  2.1 0.9 copy-start.6
  2.2 1.6 copy-start.4
  3.9 0.9 copy-start.7
  3.9 1.7 copy-start.2
  4.8 0.8 copy-start.3
  5.6 47.5 %copy-start.5 = (bf16[512,224]{0,1:T(8,128)(2,1)S(1)}, bf16[512,224]{0,1:T(8,128)(2,1)}, u32[]{:S(2)}) copy-start(bf16[512,224]{0,1:T(8,128)(2,1)} %param.18) | copy-start | bytes 688132
  110.5 1.6 copy-start.8
  110.5 2.3 %copy-start = (bf16[1,224,2048]{2,1,0:T(8,128)(2,1)S(1)}, bf16[1,224,2048]{2,1,0:T(8,128)(2,1)}, u32[]{:S(2)}) copy-start(bf16[1,224,2048]{2,1,0:T(8,128)(2,1)} %param.21) | copy-start | bytes 2752516
  112.0 0.7 copy-start.9
  112.7 1.2 copy-start.1

commit v3 on v2

v3 whole, which is shorter than its diff:
```python
import functools
import math
import types

import jax
import jax.numpy as jnp
from jax import lax
from jax.experimental import pallas as pl
from jax.experimental.pallas import tpu as pltpu
from jax.sharding import PartitionSpec as P

LAT = 512
ROPE = 64
QK_NOPE = 128
SRC_CAP = 32

EPS = 1e-06
FLOOR = -1e30
SCALE2 = (QK_NOPE + ROPE) ** (-0.5) * math.log2(math.e)
MESH = pl.DeviceIdType.MESH
VMEM = pltpu.VMEM
VMEM_BYTES = 48 * 1024 * 1024


def rdot(a, b):
    return jnp.dot(a, b, preferred_element_type=jnp.float32)


def rdot_t(a, b):
    return lax.dot_general(
        a, b, (((1,), (1,)), ((), ())), preferred_element_type=jnp.float32
    )


def rdot_tn(a, b):
    return lax.dot_general(
        a, b, (((0,), (0,)), ((), ())), preferred_element_type=jnp.float32
    )


def place(zs):
    s = lax.axis_index("seq")
    z, c = s // 2, lax.rem(s, 2)
    above = lax.rem(z + 1, zs) * 2 + c
    below = lax.rem(z + zs - 1, zs) * 2 + c
    twin = 2 * z + 1 - c
    return z, c, above, below, twin


def greet(zs, reach, peers):
    z, c, _, _, twin = place(zs)
    s = 2 * z + c
    e = lax.axis_index("exp")
    barrier = pltpu.get_barrier_semaphore()

    def hello(seq, exp):
        pl.semaphore_signal(
            barrier, inc=1, device_id={"seq": seq, "exp": exp}, device_id_type=MESH
        )

    def along(j, carry):
        hello(s, lax.rem(e + j, peers))
        return carry

    lax.fori_loop(1, peers, along, 0)
    for k in range(1, reach + 1):
        hello(lax.rem(z + k, zs) * 2 + c, e)
        hello(lax.rem(z + zs - k, zs) * 2 + c, e)
    hello(twin, e)
    return lambda: pl.semaphore_wait(barrier, 1 + 2 * reach + peers - 1)


def remote(src, dst, ssem, rsem, seq, exp):
    return pltpu.make_async_remote_copy(
        src_ref=src,
        dst_ref=dst,
        send_sem=ssem,
        recv_sem=rsem,
        device_id={"seq": seq, "exp": exp},
        device_id_type=MESH,
    )


def ring_sems(zs, parts):
    dma = pltpu.SemaphoreType.DMA
    return [dma((zs, parts)), dma((zs, parts)), dma((zs,)), dma((zs,))]


def ring_gather(
    zs, buf, sems, own, visit, stride=1, parts=1, after=None, delay=0, meanwhile=None
):
    rs, rr, ts, tr = sems
    up, down = zs // 2, zs // 2 - 1
    z, c, _, _, twin = place(zs)
    e = lax.axis_index("exp")
    size = buf.shape[1] // parts

    def far(side, k):
        return lax.rem(z + (zs - k if side == 0 else k), zs)

    def index(side, k):
        return k if side == 0 else up + k

    def hop(side, k, p, step):
        slot = buf.at[2 * far(side, k) + c, pl.ds(p * size, size)]
        i = index(side, k + step)
        to = lax.rem(z + (step if side == 0 else zs - step), zs) * 2 + c
        return remote(slot, slot, rs.at[i, p], rr.at[i, p], to, e)

    def came(side, k, p):
        slot = buf.at[2 * far(side, k) + c, pl.ds(p * size, size)]
        i = index(side, k)
        return remote(slot, slot, rs.at[i, p], rr.at[i, p], twin, e)

    def share(i, zb, core):
        slot = buf.at[2 * zb + core]
        return remote(slot, slot, ts.at[i], tr.at[i], twin, e)

    limits = (up, down)
    for p in range(parts):
        for k in range(1, stride + 1):
            for side in range(2):
                if k <= limits[side]:
                    hop(side, 0, p, k).start()
    share(0, z, c).start()
    if meanwhile is not None:
        meanwhile()

    def step(k, carry):
        for p in range(parts):
            for side in range(2):

                @pl.when(k <= limits[side])
                def _():
                    came(side, k, p).wait_recv()

                    @pl.when(k + stride <= limits[side])
                    def _():
                        hop(side, k, p, stride).start()

                    if p == parts - 1:
                        share(index(side, k), far(side, k), c).start()

        @pl.when(k == 1)
        def _():
            share(0, z, 1 - c).wait_recv()
            own()

        def both(j, act):
            def one(side, inner):
                @pl.when((side == 0) | (j <= down))
                def _():
                    zb = lax.rem(z + jnp.where(side == 0, zs - j, j), zs)
                    act(zb, jnp.where(side == 0, j, up + j))

                return inner

            lax.fori_loop(0, 2, one, 0)

        def arrive(zb, i):
            share(i, zb, 1 - c).wait_recv()
            visit(zb)

        @pl.when((k > 1) & (k <= up + 1))
        def _():
            both(k - 1, arrive)

        if after is not None:

            @pl.when(k == delay + 1)
            def _():
                after(z)

            @pl.when(k > delay + 1)
            def _():
                both(k - 1 - delay, lambda zb, i: after(zb))

        return carry

    lax.fori_loop(1, up + 2 + delay, step, 0)

    def settle():
        def drain(k, carry):
            for side in range(2):

                @pl.when(k <= limits[side])
                def _():
                    for p in range(parts):
                        came(side, k, p).wait_send()
                    share(index(side, k), far(side, k), c).wait_send()

            return carry

        lax.fori_loop(1, up + 1, drain, 0)
        share(0, z, c).wait_send()

    return settle


def attend(zs, peers, side, r, meanwhile):
    q_ref, buf, cbuf = r.q, r.keys, r.prefix
    best, total, acc = r.best, r.total, r.acc
    tok, width = buf.shape[1:]
    slots = cbuf.shape[1]
    rows = q_ref.shape[0]
    heads = rows // tok
    stride = 2
    up, down = zs // 2, zs // 2 - 1
    limits = (up, down)
    z, c, _, _, twin = place(zs)
    s = 2 * z + c
    e = lax.axis_index("exp")
    ey, ex = e // side, lax.rem(e, side)
    q = jnp.where(c == 0, ex, ey)
    size = tok // side

    def line(j):
        p = lax.rem(q + j, side)
        return jnp.where(c == 0, ey * side + p, p * side + ex)

    def lanes(x, fold):
        parts = [x[:, i * 128 : (i + 1) * 128] for i in range(x.shape[1] // 128)]
        return functools.reduce(fold, parts)

    def wide(x, like):
        return jnp.concatenate([x] * (like // 128), axis=1)

    def absorb(blocks, first=False):
        scores = []
        for keys, visible in blocks:
            raw = rdot_t(q_ref[...], keys)
            scores.append(raw if visible is None else jnp.where(visible, raw, FLOOR))
        top = functools.reduce(jnp.maximum, [lanes(x, jnp.maximum) for x in scores])
        top = jnp.max(top, axis=1, keepdims=True) * SCALE2
        newest = jnp.broadcast_to(top, best.shape)
        if not first:
            before = best[...]
            newest = jnp.maximum(before, newest)
            fade = jnp.exp2(before - newest)
        best[...] = newest
        weights = [jnp.exp2(x * SCALE2 - wide(newest, x.shape[1])) for x in scores]
        added = functools.reduce(jnp.add, [lanes(x, jnp.add) for x in weights])
        total[...] = added if first else total[...] * fade + added
        summed = functools.reduce(
            jnp.add,
            [
                rdot(x.astype(jnp.bfloat16), keys[:, :LAT])
                for x, (keys, _) in zip(weights, blocks)
            ],
        )
        acc[...] = summed if first else acc[...] * wide(fade, LAT) + summed

    def pair(zb):
        return buf[pl.ds(2 * zb, 2)].reshape(2 * tok, width)

    def far(way, k):
        return lax.rem(z + (zs - k if way == 0 else k), zs)

    def index(way, k):
        return k if way == 0 else up + k

    def piece(zb, p):
        return buf.at[2 * zb + c, pl.ds(pl.multiple_of(p * size, size), size)]

    def hop(way, k, step):
        i = index(way, k + step)
        to = lax.rem(z + (step if way == 0 else zs - step), zs) * 2 + c
        slot = piece(far(way, k), q)
        return remote(slot, slot, r.rs.at[i], r.rr.at[i], to, e)

    def cache_hop(way, k, step):
        i = index(way, k + step)
        to = lax.rem(z + (step if way == 0 else zs - step), zs) * 2 + c
        slot = cbuf.at[2 * far(way, k) + c]
        return remote(slot, slot, r.cs.at[i], r.cr.at[i], to, e)

    def came(way, k):
        i = index(way, k)
        slot = piece(far(way, k), q)
        return remote(slot, slot, r.rs.at[i], r.rr.at[i], twin, e)

    def cache_came(way, k):
        i = index(way, k)
        slot = cbuf.at[2 * far(way, k) + c]
        return remote(slot, slot, r.cs.at[i], r.cr.at[i], twin, e)

    def spread(i, zb, j):
        slot = piece(zb, q)
        return remote(slot, slot, r.ls.at[i, j], r.lr.at[i, j], s, line(j))

    def spread_in(i, zb, j):
        slot = piece(zb, lax.rem(q + side - j, side))
        return remote(slot, slot, r.ls.at[i, j], r.lr.at[i, j], s, line(j))

    def cache_spread(i, zb, j):
        slot = cbuf.at[2 * zb + c]
        return remote(slot, slot, r.ms.at[i, j], r.mr.at[i], s, line(j))

    def share(i, zb, core):
        slot = buf.at[2 * zb + core]
        return remote(slot, slot, r.ts.at[i], r.tr.at[i], twin, e)

    def cache_share(i, zb, core):
        slot = cbuf.at[2 * zb + core]
        return remote(slot, slot, r.ns.at[i], r.nr.at[i], twin, e)

    def carries(zb):
        return lax.rem(zb, side) == q

    for k in range(1, stride + 1):
        for way in range(2):
            if k <= limits[way]:
                hop(way, 0, k).start()

                @pl.when(carries(z))
                def _():
                    cache_hop(way, 0, k).start()

    share(0, z, c).start()
    cache_share(0, z, c).start()
    meanwhile()

    def step(k, carry):
        for way in range(2):
            zb, i = far(way, k), index(way, k)

            @pl.when(k <= limits[way])
            def _():
                came(way, k).wait_recv()

                @pl.when(k + stride <= limits[way])
                def _():
                    hop(way, k, stride).start()

                @pl.when(zb < z)
                def _():
                    for j in range(1, side):
                        spread(i, zb, j).start()

                @pl.when(carries(zb))
                def _():
                    cache_came(way, k).wait_recv()

                    @pl.when(k + stride <= limits[way])
                    def _():
                        cache_hop(way, k, stride).start()

                    for j in range(1, side):
                        cache_spread(i, zb, j).start()

        for way in range(2):
            zl, il = far(way, k - 1), index(way, k - 1)

            @pl.when((k > 1) & (k - 1 <= limits[way]))
            def _():
                @pl.when(zl < z)
                def _():
                    for j in range(1, side):
                        spread_in(il, zl, j).wait_recv()
                    share(il, zl, c).start()

                @pl.when(jnp.logical_not(carries(zl)))
                def _():
                    cache_spread(il, zl, 1).wait_recv()

                cache_share(il, zl, c).start()

        @pl.when(k == 2)
        def _():
            share(0, z, 1 - c).wait_recv()
            cache_share(0, z, 1 - c).wait_recv()
            row = lax.broadcasted_iota(jnp.int32, (rows, 2 * tok), 0)
            key = lax.broadcasted_iota(jnp.int32, (rows, 2 * tok), 1)
            absorb([(pair(z), key <= lax.rem(row, tok) + c * tok)], True)

        j = k - 2
        lower, upper = far(0, j), far(1, j)
        has_lower = (j >= 1) & (lower < z)
        has_upper = (j >= 1) & (j <= down) & (upper < z)

        @pl.when(j >= 1)
        def _():
            cache_share(j, lower, 1 - c).wait_recv()

        @pl.when((j >= 1) & (j <= down))
        def _():
            cache_share(up + j, upper, 1 - c).wait_recv()

        @pl.when(has_lower)
        def _():
            share(j, lower, 1 - c).wait_recv()

        @pl.when(has_upper)
        def _():
            share(up + j, upper, 1 - c).wait_recv()

        @pl.when(has_lower & has_upper)
        def _():
            absorb([(pair(lower), None), (pair(upper), None)])

        @pl.when(has_lower != has_upper)
        def _():
            absorb([(pair(jnp.where(has_lower, lower, upper)), None)])

        return carry

    lax.fori_loop(1, up + 3, step, 0)

    live = r.live[0]
    group = max(1, min(256, slots * 2 * zs) // slots)
    prefix = []
    for i in range(2 * zs // group):
        keys = cbuf[i * group : (i + 1) * group].reshape(group * slots, width)
        key = lax.broadcasted_iota(jnp.int32, (rows, group * slots), 1) + i * (group * slots)
        prefix.append((keys, key < live))
    absorb(prefix)

    r.vup_copy().wait()
    for h in range(heads):
        part = pl.ds(h * tok, tok)
        weight = jnp.sum(total[part, :], axis=1, keepdims=True)
        context = (acc[part, :] / weight).astype(jnp.bfloat16)
        vh = r.vup.shape[2]
        r.heads[s, :, h * vh : (h + 1) * vh] = rdot(context, r.vup[h]).astype(jnp.bfloat16)

    def settle():
        def drain(k, carry):
            for way in range(2):
                zb, i = far(way, k), index(way, k)

                @pl.when(k <= limits[way])
                def _():
                    came(way, k).wait_send()

                    @pl.when(zb < z)
                    def _():
                        for j in range(1, side):
                            spread(i, zb, j).wait_send()
                        share(i, zb, c).wait_send()

                    origin = jnp.maximum(k - stride, 0)
                    source = lax.rem(z + (zs - origin if way == 0 else origin), zs)

                    @pl.when(carries(source))
                    def _():
                        cache_came(way, k).wait_send()

                    @pl.when(carries(zb))
                    def _():
                        for j in range(1, side):
                            cache_spread(i, zb, j).wait_send()

                    cache_share(i, zb, c).wait_send()

            return carry

        lax.fori_loop(1, up + 1, drain, 0)
        share(0, z, c).wait_send()
        cache_share(0, z, c).wait_send()

    return settle


def project(zs, peers, side, r, meanwhile):
    buf, terms = r.heads, r.terms
    _, tok, inner = buf.shape
    width = r.proj.shape[0]
    z, c, _, _, _ = place(zs)
    s = 2 * z + c
    e = lax.axis_index("exp")
    ey, ex = e // side, lax.rem(e, side)

    def along_x(zb):
        to_y, to_x = zb // side, lax.rem(zb, side)
        return remote(
            terms.at[zb],
            r.row_in.at[to_y, ex],
            r.x_send.at[zb],
            r.x_recv.at[to_y, ex],
            s,
            ey * side + to_x,
        )

    def along_y(to_y):
        return remote(
            r.sums.at[to_y],
            r.col_in.at[ey],
            r.y_send.at[to_y],
            r.y_recv.at[ey],
            s,
            to_y * side + ex,
        )

    def visit(zb):
        rows = buf[pl.ds(2 * zb, 2)].reshape(2 * tok, inner)
        terms[zb] = rdot_t(rows, r.proj[...]).astype(jnp.bfloat16)

        @pl.when(lax.rem(zb, side) != ex)
        def _():
            along_x(zb).start()

    def after(zb):
        @pl.when(lax.rem(zb, side) == ex)
        def _():
            to_y = zb // side
            part = terms[zb].astype(jnp.float32)
            for j in range(1, side):
                g = lax.rem(ex + j, side)
                slot = r.row_in.at[to_y, g]
                remote(
                    slot, slot, r.x_send.at[zb], r.x_recv.at[to_y, g], s, ey * side + g
                ).wait_recv()
                part = part + r.row_in[to_y, g].astype(jnp.float32)

            @pl.when(to_y == ey)
            def _():
                r.hid[:, 0:width] += part

            @pl.when(to_y != ey)
            def _():
                r.sums[to_y] = part.astype(jnp.bfloat16)
                along_y(to_y).start()

    def first():
        r.proj_copy().wait()
        r.hid[...] = jnp.zeros_like(r.hid)
        r.hid[:, 0:width] = r.residual[...].astype(jnp.float32).T
        meanwhile()

    sems = (r.hs, r.hr, r.hts, r.htr)
    settle_ring = ring_gather(
        zs, buf, sems, lambda: visit(z), visit, parts=2, after=after, delay=2, meanwhile=first
    )

    for j in range(1, side):
        g = lax.rem(ey + j, side)
        slot = r.col_in.at[g]
        remote(slot, slot, r.y_send.at[g], r.y_recv.at[g], s, g * side + ex).wait_recv()
        r.hid[:, 0:width] += r.col_in[g].astype(jnp.float32)

    def settle():
        settle_ring()

        def drain(zb, carry):
            @pl.when(lax.rem(zb, side) != ex)
            def _():
                along_x(zb).wait_send()

            return carry

        lax.fori_loop(0, zs, drain, 0)
        for j in range(1, side):
            along_y(lax.rem(ey + j, side)).wait_send()

    return settle


def swap_exp(peers, send, recv, s_sem, r_sem, meanwhile):
    s = lax.axis_index("seq")
    e = lax.axis_index("exp")

    def copy(j, to, slot):
        return remote(send.at[to], recv.at[slot], s_sem.at[j], r_sem.at[j], s, to)

    def start(j, carry):
        copy(j, lax.rem(e + j, peers), e).start()
        return carry

    lax.fori_loop(1, peers, start, 0)
    recv[e] = send[e]
    meanwhile()

    def finish(j, carry):
        copy(j, lax.rem(e + j, peers), lax.rem(e + peers - j, peers)).wait_recv()
        return carry

    lax.fori_loop(1, peers, finish, 0)

    def settle():
        def drain(j, carry):
            copy(j, lax.rem(e + j, peers), e).wait_send()
            return carry

        lax.fori_loop(1, peers, drain, 0)

    return settle


def tables(peers, r):
    e = lax.axis_index("exp")
    block = r.pick.shape[1]
    cap = r.pack.shape[0]
    span = pl.ds(pl.multiple_of(e * block, block), block)
    named, weights = r.routes[:, span], r.weights[:, span].astype(jnp.float32)
    hits, scaled = [], []
    for x in range(peers):
        hit = named == x
        hits.append(jnp.max(jnp.where(hit, 1.0, 0.0), axis=0, keepdims=True))
        scaled.append(jnp.sum(jnp.where(hit, weights, 0.0), axis=0, keepdims=True))
    chosen = jnp.concatenate(hits, axis=0)
    before = lax.broadcasted_iota(jnp.int32, (block, block), 0)
    order = lax.broadcasted_iota(jnp.int32, (block, block), 1)
    earlier = jnp.where(before < order, 1.0, 0.0).astype(jnp.bfloat16)
    rank = rdot(chosen.astype(jnp.bfloat16), earlier)
    slot = lax.broadcasted_iota(jnp.int32, (SRC_CAP, block), 0).astype(jnp.float32)
    for x in range(peers):
        part = pl.ds(x * SRC_CAP, SRC_CAP)
        here = jnp.where((rank[x : x + 1] == slot) & (hits[x] > 0.0), 1.0, 0.0)
        r.pick[part, :] = here.astype(jnp.bfloat16)
        r.mix[part, :] = (here * scaled[x]).astype(jnp.bfloat16)
    mine = jnp.sum(jnp.where(r.routes[...] == e, 1.0, 0.0), axis=0, keepdims=True)
    mine = [mine[:, x * block : (x + 1) * block] for x in range(peers)]
    count = jnp.sum(jnp.concatenate(mine, axis=0), axis=1, keepdims=True)
    spots = peers * SRC_CAP
    lane = lax.broadcasted_iota(jnp.int32, (peers, spots), 1) // SRC_CAP
    source = lax.broadcasted_iota(jnp.int32, (peers, spots), 0)
    own = jnp.sum(jnp.where(lane == source, count, 0.0), axis=0, keepdims=True)
    start = jnp.sum(jnp.where(lane > source, count, 0.0), axis=0, keepdims=True)
    turn = lax.rem(lax.broadcasted_iota(jnp.int32, (1, spots), 1), SRC_CAP).astype(jnp.float32)
    at = jnp.where(turn < own, start + turn, -1.0)
    row = lax.broadcasted_iota(jnp.int32, (cap, spots), 0).astype(jnp.float32)
    r.pack[...] = jnp.where(row == at, 1.0, 0.0).astype(jnp.bfloat16)


def split_rows(v):
    row = lax.broadcasted_iota(jnp.int32, v.shape, 0)
    high = v.astype(jnp.bfloat16).astype(jnp.float32)
    rest = v - high
    mid = rest.astype(jnp.bfloat16).astype(jnp.float32)
    low = rest - mid
    parts = jnp.where(row == 0, high, jnp.where(row == 1, mid, jnp.where(row == 2, low, 0.0)))
    return parts.astype(jnp.bfloat16)


def join_rows(block):
    return jnp.sum(block.astype(jnp.float32), axis=0, keepdims=True)


def route(zs, peers, features, r, meanwhile):
    width, tokens = r.residual.shape
    wide = r.hid.shape[1]
    cap = r.pack.shape[0]
    half = cap // 2
    cols = r.ibuf.shape[2]
    up, down = zs // 2, zs // 2 - 1
    z, c, above, below, twin = place(zs)
    e = lax.axis_index("exp")

    hidden = r.hid[...]
    squares = jnp.sum(hidden * hidden, axis=1, keepdims=True)
    high = squares.astype(jnp.bfloat16).astype(jnp.float32)
    rest = squares - high
    mid = rest.astype(jnp.bfloat16).astype(jnp.float32)
    low = rest - mid
    lane = lax.broadcasted_iota(jnp.int32, (tokens, wide), 1)
    ext = jnp.where(
        lane < width,
        hidden * r.gain[...],
        jnp.where(
            lane == width,
            high,
            jnp.where(lane == width + 1, mid, jnp.where(lane == width + 2, low, 0.0)),
        ),
    ).astype(jnp.bfloat16)
    r.d_send[...] = rdot(r.pick[...], ext).astype(jnp.bfloat16).reshape(r.d_send.shape)
    settle_rows = swap_exp(peers, r.d_send, r.d_recv, r.ds_sem, r.dr_sem, meanwhile)

    arrived = r.d_recv[...].reshape(peers * SRC_CAP, wide)
    packed = rdot(r.pack[...], arrived).astype(jnp.bfloat16)
    r.xs[...] = packed
    mark = lax.broadcasted_iota(jnp.int32, (16, wide), 1)
    ones = jnp.where((mark >= width) & (mark < width + 3), 1.0, 0.0).astype(jnp.bfloat16)
    r.sqv[...] = jnp.zeros_like(r.sqv)
    r.sqv[:, 0:cap] = rdot_t(ones, packed)
    own_sq = r.sqv[...]
    tail = split_rows(own_sq)
    r.xo[0:half, :] = r.xs[pl.ds(pl.multiple_of(c * half, 16), half), 0:width]
    r.xo[half:cap, :] = r.xs[pl.ds(pl.multiple_of((1 - c) * half, 16), half), 0:width]

    def to_twin(d):
        return pltpu.make_async_remote_copy(
            src_ref=r.other.at[d],
            dst_ref=r.theirs.at[d],
            send_sem=r.ps_sem.at[d],
            recv_sem=r.pr_sem.at[d],
            device_id={"seq": twin, "exp": e},
            device_id_type=MESH,
        )

    def partial(d):
        r.load(d, 0).wait()
        r.load(d, 1).wait()
        both = rdot(r.xo[...], r.wgu[d])
        r.other[d, 0:half, :] = both[half:].astype(jnp.bfloat16)
        r.other[d, half : half + 16, :] = tail
        to_twin(d).start()
        r.mine[d] = both[:half]

    def up_copy(t):
        return pltpu.make_async_remote_copy(
            src_ref=r.up_out.at[t],
            dst_ref=r.up_in.at[t],
            send_sem=r.us_sem.at[t],
            recv_sem=r.ur_sem.at[t],
            device_id={"seq": above, "exp": e},
            device_id_type=MESH,
        )

    def dn_copy(t):
        return pltpu.make_async_remote_copy(
            src_ref=r.dn_out.at[t],
            dst_ref=r.dn_in.at[t],
            send_sem=r.ls_sem.at[t],
            recv_sem=r.lr_sem.at[t],
            device_id={"seq": below, "exp": e},
            device_id_type=MESH,
        )

    def pair_sum(d):
        to_twin(d).wait_recv()
        body = r.mine[d] + r.theirs[d, 0:half, :].astype(jnp.float32)
        sq = own_sq + join_rows(r.theirs[d, half : half + 16, :])
        return body, sq

    def relay(d, out, into, copy, t, first):
        body, sq = pair_sum(d)
        if not first:
            copy(t - 1).wait_recv()
            body = body + into[t - 1, 0:half, :].astype(jnp.float32)
            sq = sq + join_rows(into[t - 1, half : half + 16, :])
        out[t, 0:half, :] = body.astype(jnp.bfloat16)
        out[t, half : half + 16, :] = split_rows(sq)
        copy(t).start()

    def up_dest(t):
        return lax.rem(z + up - t, zs)

    def dn_dest(t):
        return lax.rem(z + zs - down + t, zs)

    partial(up_dest(0))
    partial(dn_dest(0))
    partial(up_dest(1))
    partial(dn_dest(1))
    relay(up_dest(0), r.up_out, r.up_in, up_copy, 0, True)
    relay(dn_dest(0), r.dn_out, r.dn_in, dn_copy, 0, True)

    def ring(t, carry):
        @pl.when(t < up - 1)
        def _():
            partial(up_dest(t + 1))
            partial(dn_dest(t + 1))

        relay(up_dest(t), r.up_out, r.up_in, up_copy, t, False)

        @pl.when(t < down)
        def _():
            relay(dn_dest(t), r.dn_out, r.dn_in, dn_copy, t, False)

        return carry

    lax.fori_loop(1, up, ring, 0)

    body, sq = pair_sum(z)
    up_copy(up - 1).wait_recv()
    dn_copy(down - 1).wait_recv()
    body = (
        body
        + r.up_in[up - 1, 0:half, :].astype(jnp.float32)
        + r.dn_in[down - 1, 0:half, :].astype(jnp.float32)
    )
    sq = (
        sq
        + join_rows(r.up_in[up - 1, half : half + 16, :])
        + join_rows(r.dn_in[down - 1, half : half + 16, :])
    )
    factor = lax.rsqrt(sq[0:1, :] / features + EPS)
    row = lax.broadcasted_iota(jnp.int32, (half, wide), 0) + c * half
    lane = lax.broadcasted_iota(jnp.int32, (half, wide), 1)
    factor = jnp.sum(jnp.where(row == lane, factor, 0.0), axis=1, keepdims=True)
    gate = body[:, 0:cols] * factor
    lift = body[:, cols : 2 * cols] * factor
    r.ibuf[2 * z + c] = (gate / (1.0 + jnp.exp(-gate)) * lift).astype(jnp.bfloat16)

    r.produced[...] = jnp.zeros_like(r.produced)

    def visit(zb):
        block = r.ibuf[pl.ds(2 * zb, 2)].reshape(cap, cols)
        span = pl.ds(pl.multiple_of(zb * cols, cols), cols)
        r.produced[...] += rdot_t(block, r.wd[:, span])

    def settle_sums():
        settle_rows()

        def drain(d, carry):
            to_twin(d).wait_send()
            return carry

        lax.fori_loop(0, zs, drain, 0)

        def drain_ring(t, carry):
            up_copy(t).wait_send()

            @pl.when(t < down)
            def _():
                dn_copy(t).wait_send()

            return carry

        lax.fori_loop(0, up, drain_ring, 0)
        r.wd_copy().wait()

    sems = (r.is_, r.ir, r.its, r.itr)
    settle_ring = ring_gather(
        zs, r.ibuf, sems, lambda: visit(z), visit, stride=2, meanwhile=settle_sums
    )

    produced = r.produced[...].astype(jnp.bfloat16)
    r.c_send[...] = rdot_tn(r.pack[...], produced).astype(jnp.bfloat16).reshape(r.c_send.shape)
    settle_back = swap_exp(peers, r.c_send, r.c_recv, r.cs_sem, r.cr_sem, settle_ring)
    back = r.c_recv[...].reshape(peers * SRC_CAP, width)
    r.out[...] = (r.hid[:, 0:width] + rdot_tn(r.mix[...], back)).astype(jnp.bfloat16)
    settle_back()


def layer_kernel(zs, peers, side, features, names, *refs):
    r = types.SimpleNamespace(**dict(zip(names, refs)))
    z, c, _, _, _ = place(zs)
    s = 2 * z + c
    cols = r.ibuf.shape[2]
    up, down = zs // 2, zs // 2 - 1

    def load(d, which):
        span = pl.ds(pl.multiple_of(d * cols, cols), cols)
        return pltpu.make_async_copy(
            (r.wg_hbm, r.wu_hbm)[which].at[:, span],
            r.wgu.at[d, :, pl.ds(which * cols, cols)],
            r.w_sem.at[d, which],
        )

    def load_all(d, carry):
        load(d, 0).start()
        load(d, 1).start()
        return carry

    r.load = load
    r.vup_copy = lambda: pltpu.make_async_copy(r.vup_hbm, r.vup, r.b_sem.at[0])
    r.proj_copy = lambda: pltpu.make_async_copy(r.proj_hbm, r.proj, r.b_sem.at[1])
    r.wd_copy = lambda: pltpu.make_async_copy(r.wd_hbm, r.wd, r.b_sem.at[2])
    greeted = greet(zs, 2, peers)
    r.keys[s] = r.latents[...]
    r.prefix[s] = r.cache[...]
    r.vup_copy().start()
    r.proj_copy().start()
    r.wd_copy().start()
    lax.fori_loop(0, zs, load_all, 0)
    greeted()
    settle = attend(zs, peers, side, r, lambda: tables(peers, r))
    settle = project(zs, peers, side, r, settle)
    route(zs, peers, features, r, settle)


def local(
    zs,
    peers,
    queries,
    latents,
    cache,
    prefix_len,
    value_up,
    out_proj,
    residual,
    norm_gain,
    w_gate,
    w_up,
    w_down,
    routes,
    route_weights,
):
    bf16, f32 = jnp.bfloat16, jnp.float32
    dma = pltpu.SemaphoreType.DMA
    tok, heads, qwidth = queries.shape
    slots = cache.shape[0]
    block, width = residual.shape
    inner = out_proj.shape[0]
    cap = SRC_CAP * min(peers, 6)
    half = cap // 2
    wide = -(-(width + 3) // 128) * 128
    cols = w_gate.shape[2] // zs
    up, down = zs // 2, zs // 2 - 1
    features = width * 2 * zs
    rows = tok * heads
    side = math.isqrt(peers)

    q = jnp.swapaxes(queries, 0, 1).reshape(rows, qwidth)
    operands = dict(
        q=(q, VMEM),
        latents=(latents, VMEM),
        cache=(cache, VMEM),
        live=(prefix_len, pltpu.SMEM),
        residual=(residual.T, VMEM),
        gain=(jnp.pad(norm_gain, (0, wide - width)).reshape(1, wide), VMEM),
        routes=(routes.T, VMEM),
        weights=(route_weights.T, VMEM),
        vup_hbm=(value_up, pl.ANY),
        proj_hbm=(out_proj.T, pl.ANY),
        wg_hbm=(w_gate[0], pl.ANY),
        wu_hbm=(w_up[0], pl.ANY),
        wd_hbm=(w_down[0].T, pl.ANY),
    )
    scratch = dict(
        keys=VMEM((2 * zs, tok, qwidth), bf16),
        prefix=VMEM((2 * zs, slots, qwidth), bf16),
        best=VMEM((rows, 128), f32),
        total=VMEM((rows, 128), f32),
        acc=VMEM((rows, LAT), f32),
        vup=VMEM(value_up.shape, bf16),
        rs=dma((zs,)),
        rr=dma((zs,)),
        cs=dma((zs,)),
        cr=dma((zs,)),
        ls=dma((zs, side)),
        lr=dma((zs, side)),
        ms=dma((zs, side)),
        mr=dma((zs,)),
        ts=dma((zs,)),
        tr=dma((zs,)),
        ns=dma((zs,)),
        nr=dma((zs,)),
        heads=VMEM((2 * zs, tok, inner), bf16),
        proj=VMEM((width, inner), bf16),
        terms=VMEM((peers, block, width), bf16),
        row_in=VMEM((side, side, block, width), bf16),
        sums=VMEM((side, block, width), bf16),
        col_in=VMEM((side, block, width), bf16),
        hid=VMEM((block, wide), f32),
        x_send=dma((peers,)),
        x_recv=dma((side, side)),
        y_send=dma((side,)),
        y_recv=dma((side,)),
        **dict(zip(("hs", "hr", "hts", "htr"), ring_sems(zs, 2))),
        pick=VMEM((peers * SRC_CAP, block), bf16),
        mix=VMEM((peers * SRC_CAP, block), bf16),
        pack=VMEM((cap, peers * SRC_CAP), bf16),
        wgu=VMEM((zs, width, 2 * cols), bf16),
        wd=VMEM((width, w_down.shape[1]), bf16),
        d_send=VMEM((peers, SRC_CAP, wide), bf16),
        d_recv=VMEM((peers, SRC_CAP, wide), bf16),
        xs=VMEM((cap, wide), bf16),
        xo=VMEM((cap, width), bf16),
        sqv=VMEM((16, 2 * cols), f32),
        mine=VMEM((zs, half, 2 * cols), f32),
        other=VMEM((zs, half + 16, 2 * cols), bf16),
        theirs=VMEM((zs, half + 16, 2 * cols), bf16),
        up_out=VMEM((up, half + 16, 2 * cols), bf16),
        up_in=VMEM((up, half + 16, 2 * cols), bf16),
        dn_out=VMEM((down, half + 16, 2 * cols), bf16),
        dn_in=VMEM((down, half + 16, 2 * cols), bf16),
        ibuf=VMEM((2 * zs, half, cols), bf16),
        produced=VMEM((cap, width), f32),
        c_send=VMEM((peers, SRC_CAP, width), bf16),
        c_recv=VMEM((peers, SRC_CAP, width), bf16),
        w_sem=dma((zs, 2)),
        b_sem=dma((3,)),
        ds_sem=dma((peers,)),
        dr_sem=dma((peers,)),
        ps_sem=dma((zs,)),
        pr_sem=dma((zs,)),
        us_sem=dma((up,)),
        ur_sem=dma((up,)),
        ls_sem=dma((down,)),
        lr_sem=dma((down,)),
        cs_sem=dma((peers,)),
        cr_sem=dma((peers,)),
        **dict(zip(("is_", "ir", "its", "itr"), ring_sems(zs, 1))),
    )
    names = [*operands, "out", *scratch]
    return pl.pallas_call(
        functools.partial(layer_kernel, zs, peers, side, features, names),
        out_shape=jax.ShapeDtypeStruct((block, width), bf16),
        in_specs=[pl.BlockSpec(memory_space=space) for _, space in operands.values()],
        out_specs=pl.BlockSpec(memory_space=VMEM),
        scratch_shapes=list(scratch.values()),
        compiler_params=pltpu.CompilerParams(
            collective_id=1, has_side_effects=True, vmem_limit_bytes=VMEM_BYTES
        ),
    )(*[value for value, _ in operands.values()])


def solution(mesh):
    in_specs = (
        P("seq", "exp", None),
        P("seq", None),
        P("seq", None),
        P(),
        P("exp", None, None),
        P("exp", "seq"),
        P("exp", "seq"),
        P("seq"),
        P("exp", "seq", None),
        P("exp", "seq", None),
        P("exp", None, "seq"),
        P(),
        P(),
    )
    zs, peers = mesh.shape["seq"] // 2, mesh.shape["exp"]
    return jax.shard_map(
        functools.partial(local, zs, peers),
        mesh=mesh,
        in_specs=in_specs,
        out_specs=P("exp", "seq"),
        check_vma=False,
    )
```

time: 187 us -> 175 us (0.936)
  Pallas kernels: 177 us -> 164 us
  local copies, waits for them, and re-layouts: 7.55 us -> 9.69 us
    pallas_call x3 -> x1, Pallas kernels: 177 us -> 164 us  [local(): pl.pallas_call(functools.partial(layer_kernel, zs, peers, side, features,...]
    unnamed x24 -> x19, local copies, waits for them, and re-layouts: 4.98 us -> 6.83 us
where the time goes in v3:
time: 175 us; the launch traced here: 174 us
  Pallas kernels  164 us (94%)
  local copies, waits for them, and re-layouts  9.69 us (6%)
    pallas_call x1, Pallas kernels, local(): pl.pallas_call(functools.partial(layer_kernel, zs, peers, side, features,...  164 us
    unnamed x19, local copies, waits for them, and re-layouts  6.83 us

profile of v3, /device:TPU:1, one launch (start us, length us, event | category | flops | bytes accessed | tf_op | source)
XLA Modules:
  0.0 174.1 jit_solution(17838232594720033666)
XLA Ops:
  0.0 0.0 copy-start
  0.7 0.7 pad.4
  1.4 1.1 copy.15.refs_1_
  2.5 0.0 copy-start.3
  2.5 0.0 copy-start.5
  2.5 1.4 copy.14
  3.9 0.0 copy-done
  3.9 0.0 copy-done.3
  3.9 0.0 copy-done.5
  4.0 0.0 copy-start.1
  4.0 1.2 copy-done.1
  5.1 0.0 copy-start.2
  5.1 1.2 copy-done.2
  6.3 0.0 copy-start.4
  6.3 0.9 copy-done.4
  7.3 0.0 copy-start.6
  7.3 0.9 copy-done.6
  8.2 0.0 copy-start.7
  8.2 0.8 copy-done.7
  9.0 0.0 copy-start.8
  9.0 0.7 copy-done.8
  9.7 163.7 %shard_map.127 = bf16[256,224]{1,0:T(8,128)(2,1)S(1)} custom-call(bf16[512,576]{1,0:T(8,128)(2,1)S(1)} %bitcast.12, bf16[128,576]{1,0:T(8,128)(2,1)S(1)} %copy.15.refs_1_, bf16[16,576]{1,0:T(8,128)(2,1)S(1)} %copy-done.8, s32[1]{0:T(128)S(6)} %copy.17.refs_3_, bf16[224,256]{1,0:T(8,128)(2,1)S(1)} %bitcast.18, f32[1,256]{1,0:T(1,128)S(1)} %bitcast.20, ...), custom_call_target="tpu_custom_call" | custom-call | tf_op jit(solution)/shard_map/pallas_call | solution.py:978
  173.4 0.8 copy.16
Async XLA Ops:
  0.0 3.9 %copy-start = (bf16[1,224,2048]{2,1,0:T(8,128)(2,1)S(1)}, bf16[1,224,2048]{2,1,0:T(8,128)(2,1)}, u32[]{:S(2)}) copy-start(bf16[1,224,2048]{2,1,0:T(8,128)(2,1)} %param.21) | copy-start | bytes 2752516
  2.5 1.5 copy-start.3
  2.5 1.5 copy-start.5
  4.0 1.2 copy-start.1
  5.1 1.2 copy-start.2
  6.3 0.9 copy-start.4
  7.3 0.9 copy-start.6
  8.2 0.8 copy-start.7
  9.0 0.7 copy-start.8

commit v4 on v3

--- a/solution.py
+++ b/solution.py
@@ -19,7 +19,7 @@
 SCALE2 = (QK_NOPE + ROPE) ** (-0.5) * math.log2(math.e)
 MESH = pl.DeviceIdType.MESH
 VMEM = pltpu.VMEM
-VMEM_BYTES = 48 * 1024 * 1024
+VMEM_BYTES = 60 * 1024 * 1024
 
 
 def rdot(a, b):
@@ -36,6 +36,10 @@
     return lax.dot_general(
         a, b, (((0,), (0,)), ((), ())), preferred_element_type=jnp.float32
     )
+
+
+def turn(x):
+    return x.astype(jnp.float32).T.astype(jnp.bfloat16)
 
 
 def place(zs):
@@ -201,9 +205,10 @@
     q_ref, buf, cbuf = r.q, r.keys, r.prefix
     best, total, acc = r.best, r.total, r.acc
     tok, width = buf.shape[1:]
-    slots = cbuf.shape[1]
+    slots = cbuf.shape[2]
     rows = q_ref.shape[0]
     heads = rows // tok
+    hand, use = 2, 4
     stride = 2
     up, down = zs // 2, zs // 2 - 1
     limits = (up, down)
@@ -271,7 +276,7 @@
     def cache_hop(way, k, step):
         i = index(way, k + step)
         to = lax.rem(z + (step if way == 0 else zs - step), zs) * 2 + c
-        slot = cbuf.at[2 * far(way, k) + c]
+        slot = cbuf.at[c, far(way, k)]
         return remote(slot, slot, r.cs.at[i], r.cr.at[i], to, e)
 
     def came(way, k):
@@ -281,7 +286,7 @@
 
     def cache_came(way, k):
         i = index(way, k)
-        slot = cbuf.at[2 * far(way, k) + c]
+        slot = cbuf.at[c, far(way, k)]
         return remote(slot, slot, r.cs.at[i], r.cr.at[i], twin, e)
 
     def spread(i, zb, j):
@@ -293,16 +298,16 @@
         return remote(slot, slot, r.ls.at[i, j], r.lr.at[i, j], s, line(j))
 
     def cache_spread(i, zb, j):
-        slot = cbuf.at[2 * zb + c]
+        slot = cbuf.at[c, zb]
         return remote(slot, slot, r.ms.at[i, j], r.mr.at[i], s, line(j))
 
     def share(i, zb, core):
         slot = buf.at[2 * zb + core]
         return remote(slot, slot, r.ts.at[i], r.tr.at[i], twin, e)
 
-    def cache_share(i, zb, core):
-        slot = cbuf.at[2 * zb + core]
-        return remote(slot, slot, r.ns.at[i], r.nr.at[i], twin, e)
+    def cache_share(core):
+        slot = cbuf.at[core]
+        return remote(slot, slot, r.ns.at[0], r.nr.at[0], twin, e)
 
     def carries(zb):
         return lax.rem(zb, side) == q
@@ -317,7 +322,6 @@
                     cache_hop(way, 0, k).start()
 
     share(0, z, c).start()
-    cache_share(0, z, c).start()
     meanwhile()
 
     def step(k, carry):
@@ -349,9 +353,9 @@
                         cache_spread(i, zb, j).start()
 
         for way in range(2):
-            zl, il = far(way, k - 1), index(way, k - 1)
-
-            @pl.when((k > 1) & (k - 1 <= limits[way]))
+            zl, il = far(way, k - hand), index(way, k - hand)
+
+            @pl.when((k > hand) & (k - hand <= limits[way]))
             def _():
                 @pl.when(zl < z)
                 def _():
@@ -363,29 +367,22 @@
                 def _():
                     cache_spread(il, zl, 1).wait_recv()
 
-                cache_share(il, zl, c).start()
+        @pl.when(k == up + hand)
+        def _():
+            cache_share(c).start()
 
         @pl.when(k == 2)
         def _():
             share(0, z, 1 - c).wait_recv()
-            cache_share(0, z, 1 - c).wait_recv()
             row = lax.broadcasted_iota(jnp.int32, (rows, 2 * tok), 0)
             key = lax.broadcasted_iota(jnp.int32, (rows, 2 * tok), 1)
             absorb([(pair(z), key <= lax.rem(row, tok) + c * tok)], True)
 
-        j = k - 2
+        j = k - use
         lower, upper = far(0, j), far(1, j)
         has_lower = (j >= 1) & (lower < z)
         has_upper = (j >= 1) & (j <= down) & (upper < z)
 
-        @pl.when(j >= 1)
-        def _():
-            cache_share(j, lower, 1 - c).wait_recv()
-
-        @pl.when((j >= 1) & (j <= down))
-        def _():
-            cache_share(up + j, upper, 1 - c).wait_recv()
-
         @pl.when(has_lower)
         def _():
             share(j, lower, 1 - c).wait_recv()
@@ -404,15 +401,18 @@
 
         return carry
 
-    lax.fori_loop(1, up + 3, step, 0)
-
+    lax.fori_loop(1, up + use + 1, step, 0)
+
+    cache_share(1 - c).wait_recv()
     live = r.live[0]
-    group = max(1, min(256, slots * 2 * zs) // slots)
     prefix = []
-    for i in range(2 * zs // group):
-        keys = cbuf[i * group : (i + 1) * group].reshape(group * slots, width)
-        key = lax.broadcasted_iota(jnp.int32, (rows, group * slots), 1) + i * (group * slots)
-        prefix.append((keys, key < live))
+    cores = 1 if zs * slots % 128 == 0 else 2
+    for core in range(0, 2, cores):
+        count = cores * zs * slots
+        at = lax.broadcasted_iota(jnp.int32, (rows, count), 1)
+        own_core, rest = core + at // (zs * slots), lax.rem(at, zs * slots)
+        at = (rest // slots * 2 + own_core) * slots + lax.rem(rest, slots)
+        prefix.append((cbuf[core : core + cores].reshape(count, width), at < live))
     absorb(prefix)
 
     r.vup_copy().wait()
@@ -450,13 +450,11 @@
                         for j in range(1, side):
                             cache_spread(i, zb, j).wait_send()
 
-                    cache_share(i, zb, c).wait_send()
-
             return carry
 
         lax.fori_loop(1, up + 1, drain, 0)
         share(0, z, c).wait_send()
-        cache_share(0, z, c).wait_send()
+        cache_share(c).wait_send()
 
     return settle
 
@@ -469,88 +467,98 @@
     s = 2 * z + c
     e = lax.axis_index("exp")
     ey, ex = e // side, lax.rem(e, side)
-
-    def along_x(zb):
+    one, two = jnp.where(c == 0, ex, ey), jnp.where(c == 0, ey, ex)
+
+    def split(zb):
         to_y, to_x = zb // side, lax.rem(zb, side)
+        return jnp.where(c == 0, to_x, to_y), jnp.where(c == 0, to_y, to_x)
+
+    def column(to_one, to_two):
+        return jnp.where(c == 0, to_two * side + to_one, to_one * side + to_two)
+
+    def along_one(zb):
+        to_one, to_two = split(zb)
         return remote(
             terms.at[zb],
-            r.row_in.at[to_y, ex],
+            r.row_in.at[to_two, one],
             r.x_send.at[zb],
-            r.x_recv.at[to_y, ex],
+            r.x_recv.at[to_two, one],
             s,
-            ey * side + to_x,
+            column(to_one, two),
         )
 
-    def along_y(to_y):
+    def along_two(to_two):
         return remote(
-            r.sums.at[to_y],
-            r.col_in.at[ey],
-            r.y_send.at[to_y],
-            r.y_recv.at[ey],
+            r.sums.at[to_two],
+            r.col_in.at[two],
+            r.y_send.at[to_two],
+            r.y_recv.at[two],
             s,
-            to_y * side + ex,
+            column(one, to_two),
         )
 
     def visit(zb):
         rows = buf[pl.ds(2 * zb, 2)].reshape(2 * tok, inner)
         terms[zb] = rdot_t(rows, r.proj[...]).astype(jnp.bfloat16)
 
-        @pl.when(lax.rem(zb, side) != ex)
+        @pl.when(split(zb)[0] != one)
         def _():
-            along_x(zb).start()
+            along_one(zb).start()
 
     def after(zb):
-        @pl.when(lax.rem(zb, side) == ex)
+        to_one, to_two = split(zb)
+
+        @pl.when(to_one == one)
         def _():
-            to_y = zb // side
             part = terms[zb].astype(jnp.float32)
             for j in range(1, side):
-                g = lax.rem(ex + j, side)
-                slot = r.row_in.at[to_y, g]
+                g = lax.rem(one + j, side)
+                slot = r.row_in.at[to_two, g]
                 remote(
-                    slot, slot, r.x_send.at[zb], r.x_recv.at[to_y, g], s, ey * side + g
+                    slot, slot, r.x_send.at[zb], r.x_recv.at[to_two, g], s, column(g, two)
                 ).wait_recv()
-                part = part + r.row_in[to_y, g].astype(jnp.float32)
-
-            @pl.when(to_y == ey)
+                part = part + r.row_in[to_two, g].astype(jnp.float32)
+
+            @pl.when(to_two == two)
             def _():
                 r.hid[:, 0:width] += part
 
-            @pl.when(to_y != ey)
+            @pl.when(to_two != two)
             def _():
-                r.sums[to_y] = part.astype(jnp.bfloat16)
-                along_y(to_y).start()
+                r.sums[to_two] = part.astype(jnp.bfloat16)
+                along_two(to_two).start()
 
     def first():
         r.proj_copy().wait()
+        r.res_copy().wait()
         r.hid[...] = jnp.zeros_like(r.hid)
         r.hid[:, 0:width] = r.residual[...].astype(jnp.float32).T
         meanwhile()
 
     sems = (r.hs, r.hr, r.hts, r.htr)
     settle_ring = ring_gather(
-        zs, buf, sems, lambda: visit(z), visit, parts=2, after=after, delay=2, meanwhile=first
+        zs, buf, sems, lambda: visit(z), visit, parts=4, after=after, delay=2, meanwhile=first
     )
 
     for j in range(1, side):
-        g = lax.rem(ey + j, side)
+        g = lax.rem(two + j, side)
         slot = r.col_in.at[g]
-        remote(slot, slot, r.y_send.at[g], r.y_recv.at[g], s, g * side + ex).wait_recv()
+        remote(slot, slot, r.y_send.at[g], r.y_recv.at[g], s, column(one, g)).wait_recv()
         r.hid[:, 0:width] += r.col_in[g].astype(jnp.float32)
 
     def settle():
         settle_ring()
 
         def drain(zb, carry):
-            @pl.when(lax.rem(zb, side) != ex)
+            @pl.when(split(zb)[0] != one)
             def _():
-                along_x(zb).wait_send()
+                along_one(zb).wait_send()
 
             return carry
 
         lax.fori_loop(0, zs, drain, 0)
         for j in range(1, side):
-            along_y(lax.rem(ey + j, side)).wait_send()
+            along_two(lax.rem(two + j, side)).wait_send()
 
     return settle
 
@@ -646,6 +654,7 @@
     z, c, above, below, twin = place(zs)
     e = lax.axis_index("exp")
 
+    gain = jnp.concatenate([r.gain[...], jnp.zeros((1, wide - width), jnp.float32)], axis=1)
     hidden = r.hid[...]
     squares = jnp.sum(hidden * hidden, axis=1, keepdims=True)
     high = squares.astype(jnp.bfloat16).astype(jnp.float32)
@@ -655,7 +664,7 @@
     lane = lax.broadcasted_iota(jnp.int32, (tokens, wide), 1)
     ext = jnp.where(
         lane < width,
-        hidden * r.gain[...],
+        hidden * gain,
         jnp.where(
             lane == width,
             high,
@@ -671,11 +680,12 @@
     mark = lax.broadcasted_iota(jnp.int32, (16, wide), 1)
     ones = jnp.where((mark >= width) & (mark < width + 3), 1.0, 0.0).astype(jnp.bfloat16)
     r.sqv[...] = jnp.zeros_like(r.sqv)
-    r.sqv[:, 0:cap] = rdot_t(ones, packed)
-    own_sq = r.sqv[...]
-    tail = split_rows(own_sq)
-    r.xo[0:half, :] = r.xs[pl.ds(pl.multiple_of(c * half, 16), half), 0:width]
-    r.xo[half:cap, :] = r.xs[pl.ds(pl.multiple_of((1 - c) * half, 16), half), 0:width]
+    for h in range(2):
+        span = pl.ds(pl.multiple_of((c if h == 0 else 1 - c) * half, 16), half)
+        r.xo[h * half : (h + 1) * half, :] = r.xs[span, 0:width]
+        r.sqv[h, :, 0:half] = rdot_t(ones, r.xs[span, :])
+    own_sq = r.sqv[0]
+    tail = split_rows(r.sqv[1])
 
     def to_twin(d):
         return pltpu.make_async_remote_copy(
@@ -691,46 +701,54 @@
         r.load(d, 0).wait()
         r.load(d, 1).wait()
         both = rdot(r.xo[...], r.wgu[d])
-        r.other[d, 0:half, :] = both[half:].astype(jnp.bfloat16)
-        r.other[d, half : half + 16, :] = tail
+        for p in range(2):
+            part = both[:, p * cols : (p + 1) * cols]
+            r.other[d, p, 0:half, :] = part[half:].astype(jnp.bfloat16)
+            r.other[d, p, half : half + 16, :] = tail
+            r.mine[d, p] = part[:half]
         to_twin(d).start()
-        r.mine[d] = both[:half]
-
-    def up_copy(t):
-        return pltpu.make_async_remote_copy(
-            src_ref=r.up_out.at[t],
-            dst_ref=r.up_in.at[t],
-            send_sem=r.us_sem.at[t],
-            recv_sem=r.ur_sem.at[t],
-            device_id={"seq": above, "exp": e},
-            device_id_type=MESH,
+
+    def sent_rows(p):
+        return pl.ds(0, half + 16 if p == 0 else half)
+
+    def up_copy(t, p):
+        return remote(
+            r.up_out.at[t, p, sent_rows(p)],
+            r.up_in.at[t, p, sent_rows(p)],
+            r.us_sem.at[t, p],
+            r.ur_sem.at[t, p],
+            above,
+            e,
         )
 
-    def dn_copy(t):
-        return pltpu.make_async_remote_copy(
-            src_ref=r.dn_out.at[t],
-            dst_ref=r.dn_in.at[t],
-            send_sem=r.ls_sem.at[t],
-            recv_sem=r.lr_sem.at[t],
-            device_id={"seq": below, "exp": e},
-            device_id_type=MESH,
+    def dn_copy(t, p):
+        return remote(
+            r.dn_out.at[t, p, sent_rows(p)],
+            r.dn_in.at[t, p, sent_rows(p)],
+            r.ls_sem.at[t, p],
+            r.lr_sem.at[t, p],
+            below,
+            e,
         )
 
-    def pair_sum(d):
-        to_twin(d).wait_recv()
-        body = r.mine[d] + r.theirs[d, 0:half, :].astype(jnp.float32)
-        sq = own_sq + join_rows(r.theirs[d, half : half + 16, :])
+    def pair_sum(d, p):
+        if p == 0:
+            to_twin(d).wait_recv()
+        body = r.mine[d, p] + r.theirs[d, p, 0:half, :].astype(jnp.float32)
+        sq = own_sq + join_rows(r.theirs[d, 0, half : half + 16, :]) if p == 0 else None
         return body, sq
 
-    def relay(d, out, into, copy, t, first):
-        body, sq = pair_sum(d)
+    def relay(d, out, into, copy, t, p, first):
+        body, sq = pair_sum(d, p)
         if not first:
-            copy(t - 1).wait_recv()
-            body = body + into[t - 1, 0:half, :].astype(jnp.float32)
-            sq = sq + join_rows(into[t - 1, half : half + 16, :])
-        out[t, 0:half, :] = body.astype(jnp.bfloat16)
-        out[t, half : half + 16, :] = split_rows(sq)
-        copy(t).start()
+            copy(t - 1, p).wait_recv()
+            body = body + into[t - 1, p, 0:half, :].astype(jnp.float32)
+            if p == 0:
+                sq = sq + join_rows(into[t - 1, p, half : half + 16, :])
+        out[t, p, 0:half, :] = body.astype(jnp.bfloat16)
+        if p == 0:
+            out[t, p, half : half + 16, :] = split_rows(sq)
+        copy(t, p).start()
 
     def up_dest(t):
         return lax.rem(z + up - t, zs)
@@ -742,8 +760,9 @@
     partial(dn_dest(0))
     partial(up_dest(1))
     partial(dn_dest(1))
-    relay(up_dest(0), r.up_out, r.up_in, up_copy, 0, True)
-    relay(dn_dest(0), r.dn_out, r.dn_in, dn_copy, 0, True)
+    for p in range(2):
+        relay(up_dest(0), r.up_out, r.up_in, up_copy, 0, p, True)
+        relay(dn_dest(0), r.dn_out, r.dn_in, dn_copy, 0, p, True)
 
     def ring(t, carry):
         @pl.when(t < up - 1)
@@ -751,35 +770,39 @@
             partial(up_dest(t + 1))
             partial(dn_dest(t + 1))
 
-        relay(up_dest(t), r.up_out, r.up_in, up_copy, t, False)
-
-        @pl.when(t < down)
-        def _():
-            relay(dn_dest(t), r.dn_out, r.dn_in, dn_copy, t, False)
+        for p in range(2):
+            relay(up_dest(t), r.up_out, r.up_in, up_copy, t, p, False)
+
+            @pl.when(t < down)
+            def _():
+                relay(dn_dest(t), r.dn_out, r.dn_in, dn_copy, t, p, False)
 
         return carry
 
     lax.fori_loop(1, up, ring, 0)
 
-    body, sq = pair_sum(z)
-    up_copy(up - 1).wait_recv()
-    dn_copy(down - 1).wait_recv()
-    body = (
-        body
-        + r.up_in[up - 1, 0:half, :].astype(jnp.float32)
-        + r.dn_in[down - 1, 0:half, :].astype(jnp.float32)
-    )
-    sq = (
-        sq
-        + join_rows(r.up_in[up - 1, half : half + 16, :])
-        + join_rows(r.dn_in[down - 1, half : half + 16, :])
-    )
+    sums = []
+    for p in range(2):
+        body, added = pair_sum(z, p)
+        up_copy(up - 1, p).wait_recv()
+        dn_copy(down - 1, p).wait_recv()
+        sums.append(
+            body
+            + r.up_in[up - 1, p, 0:half, :].astype(jnp.float32)
+            + r.dn_in[down - 1, p, 0:half, :].astype(jnp.float32)
+        )
+        if p == 0:
+            sq = (
+                added
+                + join_rows(r.up_in[up - 1, p, half : half + 16, :])
+                + join_rows(r.dn_in[down - 1, p, half : half + 16, :])
+            )
     factor = lax.rsqrt(sq[0:1, :] / features + EPS)
-    row = lax.broadcasted_iota(jnp.int32, (half, wide), 0) + c * half
-    lane = lax.broadcasted_iota(jnp.int32, (half, wide), 1)
+    row = lax.broadcasted_iota(jnp.int32, (half, cols), 0)
+    lane = lax.broadcasted_iota(jnp.int32, (half, cols), 1)
     factor = jnp.sum(jnp.where(row == lane, factor, 0.0), axis=1, keepdims=True)
-    gate = body[:, 0:cols] * factor
-    lift = body[:, cols : 2 * cols] * factor
+    gate = sums[0] * factor
+    lift = sums[1] * factor
     r.ibuf[2 * z + c] = (gate / (1.0 + jnp.exp(-gate)) * lift).astype(jnp.bfloat16)
 
     r.produced[...] = jnp.zeros_like(r.produced)
@@ -799,11 +822,12 @@
         lax.fori_loop(0, zs, drain, 0)
 
         def drain_ring(t, carry):
-            up_copy(t).wait_send()
-
-            @pl.when(t < down)
-            def _():
-                dn_copy(t).wait_send()
+            for p in range(2):
+                up_copy(t, p).wait_send()
+
+                @pl.when(t < down)
+                def _():
+                    dn_copy(t, p).wait_send()
 
             return carry
 
@@ -844,18 +868,42 @@
         return carry
 
     r.load = load
-    r.vup_copy = lambda: pltpu.make_async_copy(r.vup_hbm, r.vup, r.b_sem.at[0])
-    r.proj_copy = lambda: pltpu.make_async_copy(r.proj_hbm, r.proj, r.b_sem.at[1])
-    r.wd_copy = lambda: pltpu.make_async_copy(r.wd_hbm, r.wd, r.b_sem.at[2])
+
+    def whole(src, dst, i):
+        return lambda: pltpu.make_async_copy(src, dst, r.b_sem.at[i])
+
+    latents_copy = whole(r.latents_hbm, r.latents, 0)
+    cache_copy = whole(r.cache_hbm, r.prefix.at[c, z], 1)
+    queries_copy = whole(r.queries_hbm, r.queries, 2)
+    routes_copy = whole(r.routes_hbm, r.routes, 3)
+    weights_copy = whole(r.weights_hbm, r.weights, 4)
+    r.res_copy = whole(r.residual_hbm, r.residual, 5)
+    r.vup_copy = whole(r.vup_hbm, r.vup, 6)
+    r.proj_copy = whole(r.proj_hbm, r.proj, 7)
+    r.wd_copy = whole(r.wd_hbm, r.wd, 8)
+    latents_copy().start()
+    cache_copy().start()
     greeted = greet(zs, 2, peers)
-    r.keys[s] = r.latents[...]
-    r.prefix[s] = r.cache[...]
-    r.vup_copy().start()
+    for copy in (queries_copy, routes_copy, weights_copy, r.res_copy, r.vup_copy):
+        copy().start()
     r.proj_copy().start()
     r.wd_copy().start()
     lax.fori_loop(0, zs, load_all, 0)
+    latents_copy().wait()
+    r.keys[s] = turn(r.latents[...])
+    cache_copy().wait()
     greeted()
-    settle = attend(zs, peers, side, r, lambda: tables(peers, r))
+
+    def prepare():
+        tok = r.keys.shape[1]
+        queries_copy().wait()
+        for h in range(r.queries.shape[0]):
+            r.q[h * tok : (h + 1) * tok, :] = turn(r.queries[h])
+        routes_copy().wait()
+        weights_copy().wait()
+        tables(peers, r)
+
+    settle = attend(zs, peers, side, r, prepare)
     settle = project(zs, peers, side, r, settle)
     route(zs, peers, features, r, settle)
 
@@ -892,16 +940,15 @@
     rows = tok * heads
     side = math.isqrt(peers)
 
-    q = jnp.swapaxes(queries, 0, 1).reshape(rows, qwidth)
     operands = dict(
-        q=(q, VMEM),
-        latents=(latents, VMEM),
-        cache=(cache, VMEM),
+        queries_hbm=(jnp.transpose(queries, (1, 2, 0)), pl.ANY),
+        latents_hbm=(latents.T, pl.ANY),
+        cache_hbm=(cache, pl.ANY),
         live=(prefix_len, pltpu.SMEM),
-        residual=(residual.T, VMEM),
-        gain=(jnp.pad(norm_gain, (0, wide - width)).reshape(1, wide), VMEM),
-        routes=(routes.T, VMEM),
-        weights=(route_weights.T, VMEM),
+        residual_hbm=(residual.T, pl.ANY),
+        gain=(norm_gain.reshape(1, width), VMEM),
+        routes_hbm=(routes.T, pl.ANY),
+        weights_hbm=(route_weights.T, pl.ANY),
         vup_hbm=(value_up, pl.ANY),
         proj_hbm=(out_proj.T, pl.ANY),
         wg_hbm=(w_gate[0], pl.ANY),
@@ -909,8 +956,14 @@
         wd_hbm=(w_down[0].T, pl.ANY),
     )
     scratch = dict(
+        queries=VMEM((heads, qwidth, tok), bf16),
+        latents=VMEM((qwidth, tok), bf16),
+        residual=VMEM((width, block), bf16),
+        routes=VMEM(routes.shape[::-1], jnp.int32),
+        weights=VMEM(routes.shape[::-1], bf16),
+        q=VMEM((rows, qwidth), bf16),
         keys=VMEM((2 * zs, tok, qwidth), bf16),
-        prefix=VMEM((2 * zs, slots, qwidth), bf16),
+        prefix=VMEM((2, zs, slots, qwidth), bf16),
         best=VMEM((rows, 128), f32),
         total=VMEM((rows, 128), f32),
         acc=VMEM((rows, LAT), f32),
@@ -925,8 +978,8 @@
         mr=dma((zs,)),
         ts=dma((zs,)),
         tr=dma((zs,)),
-        ns=dma((zs,)),
-        nr=dma((zs,)),
+        ns=dma((1,)),
+        nr=dma((1,)),
         heads=VMEM((2 * zs, tok, inner), bf16),
         proj=VMEM((width, inner), bf16),
         terms=VMEM((peers, block, width), bf16),
@@ -938,7 +991,7 @@
         x_recv=dma((side, side)),
         y_send=dma((side,)),
         y_recv=dma((side,)),
-        **dict(zip(("hs", "hr", "hts", "htr"), ring_sems(zs, 2))),
+        **dict(zip(("hs", "hr", "hts", "htr"), ring_sems(zs, 4))),
         pick=VMEM((peers * SRC_CAP, block), bf16),
         mix=VMEM((peers * SRC_CAP, block), bf16),
         pack=VMEM((cap, peers * SRC_CAP), bf16),
@@ -948,28 +1001,28 @@
         d_recv=VMEM((peers, SRC_CAP, wide), bf16),
         xs=VMEM((cap, wide), bf16),
         xo=VMEM((cap, width), bf16),
-        sqv=VMEM((16, 2 * cols), f32),
-        mine=VMEM((zs, half, 2 * cols), f32),
-        other=VMEM((zs, half + 16, 2 * cols), bf16),
-        theirs=VMEM((zs, half + 16, 2 * cols), bf16),
-        up_out=VMEM((up, half + 16, 2 * cols), bf16),
-        up_in=VMEM((up, half + 16, 2 * cols), bf16),
-        dn_out=VMEM((down, half + 16, 2 * cols), bf16),
-        dn_in=VMEM((down, half + 16, 2 * cols), bf16),
+        sqv=VMEM((2, 16, cols), f32),
+        mine=VMEM((zs, 2, half, cols), f32),
+        other=VMEM((zs, 2, half + 16, cols), bf16),
+        theirs=VMEM((zs, 2, half + 16, cols), bf16),
+        up_out=VMEM((up, 2, half + 16, cols), bf16),
+        up_in=VMEM((up, 2, half + 16, cols), bf16),
+        dn_out=VMEM((down, 2, half + 16, cols), bf16),
+        dn_in=VMEM((down, 2, half + 16, cols), bf16),
         ibuf=VMEM((2 * zs, half, cols), bf16),
         produced=VMEM((cap, width), f32),
         c_send=VMEM((peers, SRC_CAP, width), bf16),
         c_recv=VMEM((peers, SRC_CAP, width), bf16),
         w_sem=dma((zs, 2)),
-        b_sem=dma((3,)),
+        b_sem=dma((9,)),
         ds_sem=dma((peers,)),
         dr_sem=dma((peers,)),
         ps_sem=dma((zs,)),
         pr_sem=dma((zs,)),
-        us_sem=dma((up,)),
-        ur_sem=dma((up,)),
-        ls_sem=dma((down,)),
-        lr_sem=dma((down,)),
+        us_sem=dma((up, 2)),
+        ur_sem=dma((up, 2)),
+        ls_sem=dma((down, 2)),
+        lr_sem=dma((down, 2)),
         cs_sem=dma((peers,)),
         cr_sem=dma((peers,)),
         **dict(zip(("is_", "ir", "its", "itr"), ring_sems(zs, 1))),

time: 175 us -> 159 us (0.909)
  local copies, waits for them, and re-layouts: 9.69 us -> 1.65 us
  Pallas kernels: 164 us -> 157 us
    pallas_call x1, Pallas kernels: 164 us -> 157 us  [local(): pl.pallas_call(functools.partial(layer_kernel, zs, peers, side, features,...]
    unnamed x19 -> x0, local copies, waits for them, and re-layouts: 6.83 us -> none
where the time goes in v4:
time: 159 us
  Pallas kernels  157 us (99%)
  local copies, waits for them, and re-layouts  1.65 us (1%)
    pallas_call x1, Pallas kernels, local(): pl.pallas_call(functools.partial(layer_kernel, zs, peers, side, features,...  157 us

profile of v4, /device:TPU:1, one launch (start us, length us, event | category | flops | bytes accessed | tf_op | source)
XLA Modules:
  0.0 158.9 jit_solution(7451689735024336317)
XLA Ops:
  0.7 156.5 %shard_map.127 = bf16[256,224]{1,0:T(8,128)(2,1)} custom-call(bf16[4,576,128]{2,1,0:T(8,128)(2,1)} %bitcast.15, bf16[576,128]{1,0:T(8,128)(2,1)} %bitcast.17, bf16[16,576]{1,0:T(8,128)(2,1)} %refs_2_.1, s32[1]{0:T(128)S(6)} %copy.15.refs_3_, bf16[224,256]{1,0:T(8,128)(2,1)} %bitcast.19, f32[1,224]{1,0:T(1,128)} %bitcast.21, s32[8,4096]{1,0:T(8,128)} %bitcast.18, ...), custom_call_target="tpu_custom_call" | custom-call | tf_op jit(solution)/shard_map/pallas_call | solution.py:1031
  157.2 1.7 %copy.14 = bf16[256,224]{0,1:T(8,128)(2,1)} copy(bf16[256,224]{1,0:T(8,128)(2,1)} %shard_map.127) | data formatting | bytes 229376 | tf_op jit(solution)/shard_map/pallas_call | solution.py:1031

commit v5 on v4

--- a/solution.py
+++ b/solution.py
@@ -51,7 +51,7 @@
     return z, c, above, below, twin
 
 
-def greet(zs, reach, peers):
+def greet(zs, reach, peers, side):
     z, c, _, _, twin = place(zs)
     s = 2 * z + c
     e = lax.axis_index("exp")
@@ -70,8 +70,12 @@
     for k in range(1, reach + 1):
         hello(lax.rem(z + k, zs) * 2 + c, e)
         hello(lax.rem(z + zs - k, zs) * 2 + c, e)
+    ey, ex = e // side, lax.rem(e, side)
+    for j in range(1, side):
+        hello(twin, ey * side + lax.rem(ex + j, side))
+        hello(twin, lax.rem(ey + j, side) * side + ex)
     hello(twin, e)
-    return lambda: pl.semaphore_wait(barrier, 1 + 2 * reach + peers - 1)
+    return lambda: pl.semaphore_wait(barrier, 1 + 2 * reach + peers - 1 + 2 * (side - 1))
 
 
 def remote(src, dst, ssem, rsem, seq, exp):
@@ -91,13 +95,14 @@
 
 
 def ring_gather(
-    zs, buf, sems, own, visit, stride=1, parts=1, after=None, delay=0, meanwhile=None
+    zs, buf, sems, own, visit, stride=1, parts=1, after=None, delay=0, meanwhile=None, shared=True
 ):
     rs, rr, ts, tr = sems
     up, down = zs // 2, zs // 2 - 1
     z, c, _, _, twin = place(zs)
     e = lax.axis_index("exp")
     size = buf.shape[1] // parts
+    lag = 1 if shared else 0
 
     def far(side, k):
         return lax.rem(z + (zs - k if side == 0 else k), zs)
@@ -126,7 +131,8 @@
             for side in range(2):
                 if k <= limits[side]:
                     hop(side, 0, p, k).start()
-    share(0, z, c).start()
+    if shared:
+        share(0, z, c).start()
     if meanwhile is not None:
         meanwhile()
 
@@ -142,12 +148,13 @@
                     def _():
                         hop(side, k, p, stride).start()
 
-                    if p == parts - 1:
+                    if shared and p == parts - 1:
                         share(index(side, k), far(side, k), c).start()
 
         @pl.when(k == 1)
         def _():
-            share(0, z, 1 - c).wait_recv()
+            if shared:
+                share(0, z, 1 - c).wait_recv()
             own()
 
         def both(j, act):
@@ -162,26 +169,27 @@
             lax.fori_loop(0, 2, one, 0)
 
         def arrive(zb, i):
-            share(i, zb, 1 - c).wait_recv()
+            if shared:
+                share(i, zb, 1 - c).wait_recv()
             visit(zb)
 
-        @pl.when((k > 1) & (k <= up + 1))
+        @pl.when((k > lag) & (k <= up + lag))
         def _():
-            both(k - 1, arrive)
+            both(k - lag, arrive)
 
         if after is not None:
 
-            @pl.when(k == delay + 1)
+            @pl.when(k == delay + lag)
             def _():
                 after(z)
 
-            @pl.when(k > delay + 1)
+            @pl.when(k > delay + lag)
             def _():
-                both(k - 1 - delay, lambda zb, i: after(zb))
+                both(k - lag - delay, lambda zb, i: after(zb))
 
         return carry
 
-    lax.fori_loop(1, up + 2 + delay, step, 0)
+    lax.fori_loop(1, up + 1 + lag + delay, step, 0)
 
     def settle():
         def drain(k, carry):
@@ -191,12 +199,14 @@
                 def _():
                     for p in range(parts):
                         came(side, k, p).wait_send()
-                    share(index(side, k), far(side, k), c).wait_send()
+                    if shared:
+                        share(index(side, k), far(side, k), c).wait_send()
 
             return carry
 
         lax.fori_loop(1, up + 1, drain, 0)
-        share(0, z, c).wait_send()
+        if shared:
+            share(0, z, c).wait_send()
 
     return settle
 
@@ -208,7 +218,7 @@
     slots = cbuf.shape[2]
     rows = q_ref.shape[0]
     heads = rows // tok
-    hand, use = 2, 4
+    hand, use = 2, 3
     stride = 2
     up, down = zs // 2, zs // 2 - 1
     limits = (up, down)
@@ -462,12 +472,13 @@
 def project(zs, peers, side, r, meanwhile):
     buf, terms = r.heads, r.terms
     _, tok, inner = buf.shape
-    width = r.proj.shape[0]
-    z, c, _, _, _ = place(zs)
+    width = r.proj.shape[1]
+    z, c, _, _, twin = place(zs)
     s = 2 * z + c
     e = lax.axis_index("exp")
     ey, ex = e // side, lax.rem(e, side)
     one, two = jnp.where(c == 0, ex, ey), jnp.where(c == 0, ey, ex)
+    cross = (ey, ex)
 
     def split(zb):
         to_y, to_x = zb // side, lax.rem(zb, side)
@@ -487,19 +498,20 @@
             column(to_one, two),
         )
 
-    def along_two(to_two):
+    def along_two(to_two, core):
         return remote(
-            r.sums.at[to_two],
-            r.col_in.at[two],
-            r.y_send.at[to_two],
-            r.y_recv.at[two],
-            s,
+            r.sums.at[to_two, core],
+            r.col_in.at[c, two],
+            r.y_send.at[to_two, core],
+            r.y_recv.at[c, two],
+            2 * z + core,
             column(one, to_two),
         )
 
     def visit(zb):
-        rows = buf[pl.ds(2 * zb, 2)].reshape(2 * tok, inner)
-        terms[zb] = rdot_t(rows, r.proj[...]).astype(jnp.bfloat16)
+        rows = buf[2 * zb + c]
+        for core in range(2):
+            terms[zb, core] = rdot_t(rows, r.proj[core]).astype(jnp.bfloat16)
 
         @pl.when(split(zb)[0] != one)
         def _():
@@ -510,26 +522,31 @@
 
         @pl.when(to_one == one)
         def _():
-            part = terms[zb].astype(jnp.float32)
             for j in range(1, side):
                 g = lax.rem(one + j, side)
                 slot = r.row_in.at[to_two, g]
                 remote(
                     slot, slot, r.x_send.at[zb], r.x_recv.at[to_two, g], s, column(g, two)
                 ).wait_recv()
-                part = part + r.row_in[to_two, g].astype(jnp.float32)
-
-            @pl.when(to_two == two)
-            def _():
-                r.hid[:, 0:width] += part
-
-            @pl.when(to_two != two)
-            def _():
-                r.sums[to_two] = part.astype(jnp.bfloat16)
-                along_two(to_two).start()
+            for core in range(2):
+                part = terms[zb, core].astype(jnp.float32)
+                for j in range(1, side):
+                    part = part + r.row_in[to_two, lax.rem(one + j, side), core].astype(
+                        jnp.float32
+                    )
+
+                @pl.when((to_two == two) & (core == c))
+                def _():
+                    span = pl.ds(pl.multiple_of(c * tok, tok), tok)
+                    r.hid[span, 0:width] += part
+
+                @pl.when((to_two != two) | (core != c))
+                def _():
+                    r.sums[to_two, core] = part.astype(jnp.bfloat16)
+                    along_two(to_two, core).start()
 
     def first():
-        r.proj_copy().wait()
+        r.proj_swap(1 - c).wait_recv()
         r.res_copy().wait()
         r.hid[...] = jnp.zeros_like(r.hid)
         r.hid[:, 0:width] = r.residual[...].astype(jnp.float32).T
@@ -537,17 +554,39 @@
 
     sems = (r.hs, r.hr, r.hts, r.htr)
     settle_ring = ring_gather(
-        zs, buf, sems, lambda: visit(z), visit, parts=4, after=after, delay=2, meanwhile=first
+        zs,
+        buf,
+        sems,
+        lambda: visit(z),
+        visit,
+        parts=4,
+        after=after,
+        delay=2,
+        meanwhile=first,
+        shared=False,
     )
 
-    for j in range(1, side):
-        g = lax.rem(two + j, side)
-        slot = r.col_in.at[g]
-        remote(slot, slot, r.y_send.at[g], r.y_recv.at[g], s, column(one, g)).wait_recv()
-        r.hid[:, 0:width] += r.col_in[g].astype(jnp.float32)
+    for core in range(2):
+        for j in range(side):
+            g = lax.rem(cross[core] + j, side)
+
+            def collect():
+                slot = r.col_in.at[core, g]
+                remote(
+                    slot, slot, r.y_send.at[0, 0], r.y_recv.at[core, g], 2 * z + core, e
+                ).wait_recv()
+                r.hid[core * tok : (core + 1) * tok, 0:width] += r.col_in[core, g].astype(
+                    jnp.float32
+                )
+
+            if j == 0:
+                pl.when(core != c)(collect)
+            else:
+                collect()
 
     def settle():
         settle_ring()
+        r.proj_swap(c).wait_send()
 
         def drain(zb, carry):
             @pl.when(split(zb)[0] != one)
@@ -557,8 +596,13 @@
             return carry
 
         lax.fori_loop(0, zs, drain, 0)
-        for j in range(1, side):
-            along_two(lax.rem(two + j, side)).wait_send()
+        for j in range(side):
+            for core in range(2):
+                to_two = lax.rem(two + j, side)
+
+                @pl.when((to_two != two) | (core != c))
+                def _():
+                    along_two(to_two, core).wait_send()
 
     return settle
 
@@ -879,11 +923,19 @@
     weights_copy = whole(r.weights_hbm, r.weights, 4)
     r.res_copy = whole(r.residual_hbm, r.residual, 5)
     r.vup_copy = whole(r.vup_hbm, r.vup, 6)
-    r.proj_copy = whole(r.proj_hbm, r.proj, 7)
+    r.proj_copy = whole(r.proj_hbm, r.proj.at[c], 7)
+    r.proj_swap = lambda core: remote(
+        r.proj.at[core],
+        r.proj.at[core],
+        r.o_sem.at[0],
+        r.o_sem.at[1],
+        2 * z + 1 - c,
+        lax.axis_index("exp"),
+    )
     r.wd_copy = whole(r.wd_hbm, r.wd, 8)
     latents_copy().start()
     cache_copy().start()
-    greeted = greet(zs, 2, peers)
+    greeted = greet(zs, 2, peers, side)
     for copy in (queries_copy, routes_copy, weights_copy, r.res_copy, r.vup_copy):
         copy().start()
     r.proj_copy().start()
@@ -899,6 +951,8 @@
         queries_copy().wait()
         for h in range(r.queries.shape[0]):
             r.q[h * tok : (h + 1) * tok, :] = turn(r.queries[h])
+        r.proj_copy().wait()
+        r.proj_swap(c).start()
         routes_copy().wait()
         weights_copy().wait()
         tables(peers, r)
@@ -981,16 +1035,16 @@
         ns=dma((1,)),
         nr=dma((1,)),
         heads=VMEM((2 * zs, tok, inner), bf16),
-        proj=VMEM((width, inner), bf16),
-        terms=VMEM((peers, block, width), bf16),
-        row_in=VMEM((side, side, block, width), bf16),
-        sums=VMEM((side, block, width), bf16),
-        col_in=VMEM((side, block, width), bf16),
+        proj=VMEM((2, width, inner), bf16),
+        terms=VMEM((peers, 2, tok, width), bf16),
+        row_in=VMEM((side, side, 2, tok, width), bf16),
+        sums=VMEM((side, 2, tok, width), bf16),
+        col_in=VMEM((2, side, tok, width), bf16),
         hid=VMEM((block, wide), f32),
         x_send=dma((peers,)),
         x_recv=dma((side, side)),
-        y_send=dma((side,)),
-        y_recv=dma((side,)),
+        y_send=dma((side, 2)),
+        y_recv=dma((2, side)),
         **dict(zip(("hs", "hr", "hts", "htr"), ring_sems(zs, 4))),
         pick=VMEM((peers * SRC_CAP, block), bf16),
         mix=VMEM((peers * SRC_CAP, block), bf16),
@@ -1015,6 +1069,7 @@
         c_recv=VMEM((peers, SRC_CAP, width), bf16),
         w_sem=dma((zs, 2)),
         b_sem=dma((9,)),
+        o_sem=dma((2,)),
         ds_sem=dma((peers,)),
         dr_sem=dma((peers,)),
         ps_sem=dma((zs,)),

time: 159 us -> 161 us (1.013)
    pallas_call x1, Pallas kernels: 157 us -> 158 us  [local(): pl.pallas_call(functools.partial(layer_kernel, zs, peers, side, features,...]
where the time goes in v5:
time: 161 us
  Pallas kernels  158 us (98%)
  local copies, waits for them, and re-layouts  1.65 us (1%)
    pallas_call x1, Pallas kernels, local(): pl.pallas_call(functools.partial(layer_kernel, zs, peers, side, features,...  158 us

profile of v5, /device:TPU:1, one launch (start us, length us, event | category | flops | bytes accessed | tf_op | source)
XLA Modules:
  0.0 160.5 jit_solution(18116119616565811237)
XLA Ops:
  0.7 158.2 %shard_map.127 = bf16[256,224]{1,0:T(8,128)(2,1)} custom-call(bf16[4,576,128]{2,1,0:T(8,128)(2,1)} %bitcast.15, bf16[576,128]{1,0:T(8,128)(2,1)} %bitcast.17, bf16[16,576]{1,0:T(8,128)(2,1)} %refs_2_.1, s32[1]{0:T(128)S(6)} %copy.15.refs_3_, bf16[224,256]{1,0:T(8,128)(2,1)} %bitcast.19, f32[1,224]{1,0:T(1,128)} %bitcast.21, s32[8,4096]{1,0:T(8,128)} %bitcast.18, ...), custom_call_target="tpu_custom_call" | custom-call | tf_op jit(solution)/shard_map/pallas_call | solution.py:1086
  158.9 1.7 %copy.14 = bf16[256,224]{0,1:T(8,128)(2,1)} copy(bf16[256,224]{1,0:T(8,128)(2,1)} %shard_map.127) | data formatting | bytes 229376 | tf_op jit(solution)/shard_map/pallas_call | solution.py:1086

commit v6 on v5

--- a/solution.py
+++ b/solution.py
@@ -695,7 +695,7 @@
     half = cap // 2
     cols = r.ibuf.shape[2]
     up, down = zs // 2, zs // 2 - 1
-    z, c, above, below, twin = place(zs)
+    z, c, _, _, twin = place(zs)
     e = lax.axis_index("exp")
 
     gain = jnp.concatenate([r.gain[...], jnp.zeros((1, wide - width), jnp.float32)], axis=1)
@@ -755,25 +755,27 @@
     def sent_rows(p):
         return pl.ds(0, half + 16 if p == 0 else half)
 
-    def up_copy(t, p):
+    def chunk_copy(way, d, p):
+        out, into, ssem, rsem = chains[way]
+        ahead = jnp.minimum(d, 2)
+        to = lax.rem(z + (ahead if way == 0 else zs - ahead), zs) * 2 + c
         return remote(
-            r.up_out.at[t, p, sent_rows(p)],
-            r.up_in.at[t, p, sent_rows(p)],
-            r.us_sem.at[t, p],
-            r.ur_sem.at[t, p],
-            above,
+            out.at[d - 1, p, sent_rows(p)],
+            into.at[d - 1, p, sent_rows(p)],
+            ssem.at[d - 1, p],
+            rsem.at[d - 1, p],
+            to,
             e,
         )
 
-    def dn_copy(t, p):
-        return remote(
-            r.dn_out.at[t, p, sent_rows(p)],
-            r.dn_in.at[t, p, sent_rows(p)],
-            r.ls_sem.at[t, p],
-            r.lr_sem.at[t, p],
-            below,
-            e,
-        )
+    chains = (
+        (r.up_out, r.up_in, r.us_sem, r.ur_sem),
+        (r.dn_out, r.dn_in, r.ls_sem, r.lr_sem),
+    )
+    limits = (up, down)
+
+    def end(way, d):
+        return lax.rem(z + (d if way == 0 else zs - d), zs)
 
     def pair_sum(d, p):
         if p == 0:
@@ -782,65 +784,56 @@
         sq = own_sq + join_rows(r.theirs[d, 0, half : half + 16, :]) if p == 0 else None
         return body, sq
 
-    def relay(d, out, into, copy, t, p, first):
-        body, sq = pair_sum(d, p)
+    def relay(way, d, p, first):
+        out, into, _, _ = chains[way]
+        body, sq = pair_sum(end(way, d), p)
         if not first:
-            copy(t - 1, p).wait_recv()
-            body = body + into[t - 1, p, 0:half, :].astype(jnp.float32)
+            chunk_copy(way, d + 2, p).wait_recv()
+            body = body + into[d + 1, p, 0:half, :].astype(jnp.float32)
             if p == 0:
-                sq = sq + join_rows(into[t - 1, p, half : half + 16, :])
-        out[t, p, 0:half, :] = body.astype(jnp.bfloat16)
+                sq = sq + join_rows(into[d + 1, p, half : half + 16, :])
+        out[d - 1, p, 0:half, :] = body.astype(jnp.bfloat16)
         if p == 0:
-            out[t, p, half : half + 16, :] = split_rows(sq)
-        copy(t, p).start()
-
-    def up_dest(t):
-        return lax.rem(z + up - t, zs)
-
-    def dn_dest(t):
-        return lax.rem(z + zs - down + t, zs)
-
-    partial(up_dest(0))
-    partial(dn_dest(0))
-    partial(up_dest(1))
-    partial(dn_dest(1))
-    for p in range(2):
-        relay(up_dest(0), r.up_out, r.up_in, up_copy, 0, p, True)
-        relay(dn_dest(0), r.dn_out, r.dn_in, dn_copy, 0, p, True)
+            out[d - 1, p, half : half + 16, :] = split_rows(sq)
+        chunk_copy(way, d, p).start()
+
+    def order(t):
+        return [(way, limits[way] - 2 * t - x) for x in range(2) for way in range(2)]
+
+    for way, d in order(0):
+        partial(end(way, d))
+    for way, d in order(0):
+        if d >= 1:
+            for p in range(2):
+                relay(way, d, p, True)
 
     def ring(t, carry):
-        @pl.when(t < up - 1)
-        def _():
-            partial(up_dest(t + 1))
-            partial(dn_dest(t + 1))
-
-        for p in range(2):
-            relay(up_dest(t), r.up_out, r.up_in, up_copy, t, p, False)
-
-            @pl.when(t < down)
+        for way, d in order(t):
+            partial(end(way, d))
+        for way, d in order(t):
+
+            @pl.when(d >= 1)
             def _():
-                relay(dn_dest(t), r.dn_out, r.dn_in, dn_copy, t, p, False)
+                for p in range(2):
+                    relay(way, d, p, False)
 
         return carry
 
-    lax.fori_loop(1, up, ring, 0)
+    lax.fori_loop(1, up // 2, ring, 0)
 
     sums = []
     for p in range(2):
-        body, added = pair_sum(z, p)
-        up_copy(up - 1, p).wait_recv()
-        dn_copy(down - 1, p).wait_recv()
-        sums.append(
-            body
-            + r.up_in[up - 1, p, 0:half, :].astype(jnp.float32)
-            + r.dn_in[down - 1, p, 0:half, :].astype(jnp.float32)
-        )
+        total, added = pair_sum(z, p)
+        for way in range(2):
+            for d in range(1, min(2, limits[way]) + 1):
+                into = chains[way][1]
+                chunk_copy(way, d, p).wait_recv()
+                total = total + into[d - 1, p, 0:half, :].astype(jnp.float32)
+                if p == 0:
+                    added = added + join_rows(into[d - 1, p, half : half + 16, :])
+        sums.append(total)
         if p == 0:
-            sq = (
-                added
-                + join_rows(r.up_in[up - 1, p, half : half + 16, :])
-                + join_rows(r.dn_in[down - 1, p, half : half + 16, :])
-            )
+            sq = added
     factor = lax.rsqrt(sq[0:1, :] / features + EPS)
     row = lax.broadcasted_iota(jnp.int32, (half, cols), 0)
     lane = lax.broadcasted_iota(jnp.int32, (half, cols), 1)
@@ -867,15 +860,15 @@
 
         def drain_ring(t, carry):
             for p in range(2):
-                up_copy(t, p).wait_send()
-
-                @pl.when(t < down)
-                def _():
-                    dn_copy(t, p).wait_send()
+                chunk_copy(0, t, p).wait_send()
+
+                @pl.when(t <= down)
+                def _():
+                    chunk_copy(1, t, p).wait_send()
 
             return carry
 
-        lax.fori_loop(0, up, drain_ring, 0)
+        lax.fori_loop(1, up + 1, drain_ring, 0)
         r.wd_copy().wait()
 
     sems = (r.is_, r.ir, r.its, r.itr)
@@ -887,7 +880,7 @@
     r.c_send[...] = rdot_tn(r.pack[...], produced).astype(jnp.bfloat16).reshape(r.c_send.shape)
     settle_back = swap_exp(peers, r.c_send, r.c_recv, r.cs_sem, r.cr_sem, settle_ring)
     back = r.c_recv[...].reshape(peers * SRC_CAP, width)
-    r.out[...] = (r.hid[:, 0:width] + rdot_tn(r.mix[...], back)).astype(jnp.bfloat16)
+    r.out[...] = (r.hid[:, 0:width] + rdot_tn(r.mix[...], back)).T.astype(jnp.bfloat16)
     settle_back()
 
 
@@ -1085,14 +1078,14 @@
     names = [*operands, "out", *scratch]
     return pl.pallas_call(
         functools.partial(layer_kernel, zs, peers, side, features, names),
-        out_shape=jax.ShapeDtypeStruct((block, width), bf16),
+        out_shape=jax.ShapeDtypeStruct((width, block), bf16),
         in_specs=[pl.BlockSpec(memory_space=space) for _, space in operands.values()],
         out_specs=pl.BlockSpec(memory_space=VMEM),
         scratch_shapes=list(scratch.values()),
         compiler_params=pltpu.CompilerParams(
             collective_id=1, has_side_effects=True, vmem_limit_bytes=VMEM_BYTES
         ),
-    )(*[value for value, _ in operands.values()])
+    )(*[value for value, _ in operands.values()]).T
 
 
 def solution(mesh):

time: 161 us -> 156 us (0.969)
  Pallas kernels: 158 us -> 154 us
    pallas_call x1, Pallas kernels: 158 us -> 154 us  [local(): pl.pallas_call(functools.partial(layer_kernel, zs, peers, side, features,...]
    pallas_call x1 -> x0, local copies, waits for them, and re-layouts: 1.65 us -> none  [local(): pl.pallas_call(functools.partial(layer_kernel, zs, peers, side, features,...]
where the time goes in v6:
time: 156 us
  Pallas kernels  154 us (99%)
    pallas_call x1, Pallas kernels, local(): pl.pallas_call(functools.partial(layer_kernel, zs, peers, side, features,...  154 us

profile of v6, /device:TPU:1, one launch (start us, length us, event | category | flops | bytes accessed | tf_op | source)
XLA Modules:
  0.0 155.9 jit_solution(3889388399265111856)
XLA Ops:
  0.7 153.6 %shard_map.127 = bf16[224,256]{1,0:T(8,128)(2,1)} custom-call(bf16[4,576,128]{2,1,0:T(8,128)(2,1)} %bitcast.16, bf16[576,128]{1,0:T(8,128)(2,1)} %bitcast.19, bf16[16,576]{1,0:T(8,128)(2,1)} %refs_2_.1, s32[1]{0:T(128)S(6)} %copy.15.refs_3_, bf16[224,256]{1,0:T(8,128)(2,1)} %bitcast.21, f32[1,224]{1,0:T(1,128)} %bitcast.23, s32[8,4096]{1,0:T(8,128)} %bitcast.20, ...), custom_call_target="tpu_custom_call" | custom-call | tf_op jit(solution)/shard_map/pallas_call | solution.py:1079
  154.3 1.6 copy.16

commit v7 on v6

--- a/solution.py
+++ b/solution.py
@@ -211,7 +211,7 @@
     return settle
 
 
-def attend(zs, peers, side, r, meanwhile):
+def attend(zs, peers, side, r, meanwhile, later):
     q_ref, buf, cbuf = r.q, r.keys, r.prefix
     best, total, acc = r.best, r.total, r.acc
     tok, width = buf.shape[1:]
@@ -241,29 +241,36 @@
         return jnp.concatenate([x] * (like // 128), axis=1)
 
     def absorb(blocks, first=False):
+        band = min(rows, 256)
+        spans = [slice(at, at + band) for at in range(0, rows, band)]
         scores = []
-        for keys, visible in blocks:
-            raw = rdot_t(q_ref[...], keys)
-            scores.append(raw if visible is None else jnp.where(visible, raw, FLOOR))
-        top = functools.reduce(jnp.maximum, [lanes(x, jnp.maximum) for x in scores])
-        top = jnp.max(top, axis=1, keepdims=True) * SCALE2
-        newest = jnp.broadcast_to(top, best.shape)
-        if not first:
-            before = best[...]
-            newest = jnp.maximum(before, newest)
-            fade = jnp.exp2(before - newest)
-        best[...] = newest
-        weights = [jnp.exp2(x * SCALE2 - wide(newest, x.shape[1])) for x in scores]
-        added = functools.reduce(jnp.add, [lanes(x, jnp.add) for x in weights])
-        total[...] = added if first else total[...] * fade + added
-        summed = functools.reduce(
-            jnp.add,
-            [
-                rdot(x.astype(jnp.bfloat16), keys[:, :LAT])
-                for x, (keys, _) in zip(weights, blocks)
-            ],
-        )
-        acc[...] = summed if first else acc[...] * wide(fade, LAT) + summed
+        for span in spans:
+            scores.append([])
+            for keys, visible in blocks:
+                raw = rdot_t(q_ref[span, :], keys)
+                scores[-1].append(
+                    raw if visible is None else jnp.where(visible[span], raw, FLOOR)
+                )
+        for span, held in zip(spans, scores):
+            top = functools.reduce(jnp.maximum, [lanes(x, jnp.maximum) for x in held])
+            top = jnp.max(top, axis=1, keepdims=True) * SCALE2
+            newest = jnp.broadcast_to(top, (band, best.shape[1]))
+            if not first:
+                before = best[span, :]
+                newest = jnp.maximum(before, newest)
+                fade = jnp.exp2(before - newest)
+            best[span, :] = newest
+            weights = [jnp.exp2(x * SCALE2 - wide(newest, x.shape[1])) for x in held]
+            added = functools.reduce(jnp.add, [lanes(x, jnp.add) for x in weights])
+            total[span, :] = added if first else total[span, :] * fade + added
+            summed = functools.reduce(
+                jnp.add,
+                [
+                    rdot(x.astype(jnp.bfloat16), keys[:, :LAT])
+                    for x, (keys, _) in zip(weights, blocks)
+                ],
+            )
+            acc[span, :] = summed if first else acc[span, :] * wide(fade, LAT) + summed
 
     def pair(zb):
         return buf[pl.ds(2 * zb, 2)].reshape(2 * tok, width)
@@ -336,7 +343,6 @@
 
     def step(k, carry):
         for way in range(2):
-            zb, i = far(way, k), index(way, k)
 
             @pl.when(k <= limits[way])
             def _():
@@ -346,6 +352,11 @@
                 def _():
                     hop(way, k, stride).start()
 
+        for way in range(2):
+            zb, i = far(way, k), index(way, k)
+
+            @pl.when(k <= limits[way])
+            def _():
                 @pl.when(zb < z)
                 def _():
                     for j in range(1, side):
@@ -387,6 +398,7 @@
             row = lax.broadcasted_iota(jnp.int32, (rows, 2 * tok), 0)
             key = lax.broadcasted_iota(jnp.int32, (rows, 2 * tok), 1)
             absorb([(pair(z), key <= lax.rem(row, tok) + c * tok)], True)
+            later()
 
         j = k - use
         lower, upper = far(0, j), far(1, j)
@@ -469,7 +481,7 @@
     return settle
 
 
-def project(zs, peers, side, r, meanwhile):
+def project(zs, peers, side, r):
     buf, terms = r.heads, r.terms
     _, tok, inner = buf.shape
     width = r.proj.shape[1]
@@ -547,10 +559,6 @@
 
     def first():
         r.proj_swap(1 - c).wait_recv()
-        r.res_copy().wait()
-        r.hid[...] = jnp.zeros_like(r.hid)
-        r.hid[:, 0:width] = r.residual[...].astype(jnp.float32).T
-        meanwhile()
 
     sems = (r.hs, r.hr, r.hts, r.htr)
     settle_ring = ring_gather(
@@ -946,12 +954,22 @@
             r.q[h * tok : (h + 1) * tok, :] = turn(r.queries[h])
         r.proj_copy().wait()
         r.proj_swap(c).start()
+        r.res_copy().wait()
+        r.hid[...] = jnp.zeros_like(r.hid)
+        r.hid[:, 0 : r.residual.shape[0]] = r.residual[...].astype(jnp.float32).T
+
+    def prepare_tables():
         routes_copy().wait()
         weights_copy().wait()
         tables(peers, r)
 
-    settle = attend(zs, peers, side, r, prepare)
-    settle = project(zs, peers, side, r, settle)
+    settle_keys = attend(zs, peers, side, r, prepare, prepare_tables)
+    settle_heads = project(zs, peers, side, r)
+
+    def settle():
+        settle_keys()
+        settle_heads()
+
     route(zs, peers, features, r, settle)
 
 

time: 156 us -> 156 us (level)
  no operation moved by 1% of the time
where the time goes in v7:
time: 156 us
  Pallas kernels  154 us (99%)
    pallas_call x1, Pallas kernels, local(): pl.pallas_call(functools.partial(layer_kernel, zs, peers, side, features,...  154 us

profile of v7, /device:TPU:1, one launch (start us, length us, event | category | flops | bytes accessed | tf_op | source)
XLA Modules:
  0.0 155.8 jit_solution(2924491265429796632)
XLA Ops:
  0.7 153.6 %shard_map.127 = bf16[224,256]{1,0:T(8,128)(2,1)} custom-call(bf16[4,576,128]{2,1,0:T(8,128)(2,1)} %bitcast.16, bf16[576,128]{1,0:T(8,128)(2,1)} %bitcast.19, bf16[16,576]{1,0:T(8,128)(2,1)} %refs_2_.1, s32[1]{0:T(128)S(6)} %copy.15.refs_3_, bf16[224,256]{1,0:T(8,128)(2,1)} %bitcast.21, f32[1,224]{1,0:T(1,128)} %bitcast.23, s32[8,4096]{1,0:T(8,128)} %bitcast.20, ...), custom_call_target="tpu_custom_call" | custom-call | tf_op jit(solution)/shard_map/pallas_call | solution.py:1097
  154.3 1.6 copy.16

commit v8 on v7

--- a/solution.py
+++ b/solution.py
@@ -226,12 +226,18 @@
     s = 2 * z + c
     e = lax.axis_index("exp")
     ey, ex = e // side, lax.rem(e, side)
-    q = jnp.where(c == 0, ex, ey)
-    size = tok // side
-
-    def line(j):
-        p = lax.rem(q + j, side)
-        return jnp.where(c == 0, ey * side + p, p * side + ex)
+    bx, by = lax.rem(ex + c, 2), lax.rem(ey + c, 2)
+    mate_x = lax.rem(ex + 1 - 2 * bx + side, side)
+    mate_y = lax.rem(ey + 1 - 2 * by + side, side)
+    quads = 4
+    q = 2 * by + bx
+    size = tok // quads
+
+    def member(j):
+        p = lax.rem(q + j, quads)
+        x = jnp.where(lax.rem(p, 2) == bx, ex, mate_x)
+        y = jnp.where(p // 2 == by, ey, mate_y)
+        return y * side + x
 
     def lanes(x, fold):
         parts = [x[:, i * 128 : (i + 1) * 128] for i in range(x.shape[1] // 128)]
@@ -308,15 +314,15 @@
 
     def spread(i, zb, j):
         slot = piece(zb, q)
-        return remote(slot, slot, r.ls.at[i, j], r.lr.at[i, j], s, line(j))
+        return remote(slot, slot, r.ls.at[i, j], r.lr.at[i, j], s, member(j))
 
     def spread_in(i, zb, j):
-        slot = piece(zb, lax.rem(q + side - j, side))
-        return remote(slot, slot, r.ls.at[i, j], r.lr.at[i, j], s, line(j))
+        slot = piece(zb, lax.rem(q + quads - j, quads))
+        return remote(slot, slot, r.ls.at[i, j], r.lr.at[i, j], s, member(j))
 
     def cache_spread(i, zb, j):
         slot = cbuf.at[c, zb]
-        return remote(slot, slot, r.ms.at[i, j], r.mr.at[i], s, line(j))
+        return remote(slot, slot, r.ms.at[i, j], r.mr.at[i], s, member(j))
 
     def share(i, zb, core):
         slot = buf.at[2 * zb + core]
@@ -327,7 +333,7 @@
         return remote(slot, slot, r.ns.at[0], r.nr.at[0], twin, e)
 
     def carries(zb):
-        return lax.rem(zb, side) == q
+        return lax.rem(zb, quads) == q
 
     for k in range(1, stride + 1):
         for way in range(2):
@@ -359,7 +365,7 @@
             def _():
                 @pl.when(zb < z)
                 def _():
-                    for j in range(1, side):
+                    for j in range(1, quads):
                         spread(i, zb, j).start()
 
                 @pl.when(carries(zb))
@@ -370,7 +376,7 @@
                     def _():
                         cache_hop(way, k, stride).start()
 
-                    for j in range(1, side):
+                    for j in range(1, quads):
                         cache_spread(i, zb, j).start()
 
         for way in range(2):
@@ -380,7 +386,7 @@
             def _():
                 @pl.when(zl < z)
                 def _():
-                    for j in range(1, side):
+                    for j in range(1, quads):
                         spread_in(il, zl, j).wait_recv()
                     share(il, zl, c).start()
 
@@ -456,7 +462,7 @@
 
                     @pl.when(zb < z)
                     def _():
-                        for j in range(1, side):
+                        for j in range(1, quads):
                             spread(i, zb, j).wait_send()
                         share(i, zb, c).wait_send()
 
@@ -469,7 +475,7 @@
 
                     @pl.when(carries(zb))
                     def _():
-                        for j in range(1, side):
+                        for j in range(1, quads):
                             cache_spread(i, zb, j).wait_send()
 
             return carry
@@ -1037,9 +1043,9 @@
         rr=dma((zs,)),
         cs=dma((zs,)),
         cr=dma((zs,)),
-        ls=dma((zs, side)),
-        lr=dma((zs, side)),
-        ms=dma((zs, side)),
+        ls=dma((zs, 4)),
+        lr=dma((zs, 4)),
+        ms=dma((zs, 4)),
         mr=dma((zs,)),
         ts=dma((zs,)),
         tr=dma((zs,)),

time: 156 us -> 158 us (1.013)
    pallas_call x1, Pallas kernels: 154 us -> 155 us  [local(): pl.pallas_call(functools.partial(layer_kernel, zs, peers, side, features,...]
where the time goes in v8:
time: 158 us; the launch traced here: 157 us
  Pallas kernels  155 us (98%)
    pallas_call x1, Pallas kernels, local(): pl.pallas_call(functools.partial(layer_kernel, zs, peers, side, features,...  155 us

profile of v8, /device:TPU:1, one launch (start us, length us, event | category | flops | bytes accessed | tf_op | source)
XLA Modules:
  0.0 157.5 jit_solution(9604164944560633684)
XLA Ops:
  0.7 155.3 %shard_map.127 = bf16[224,256]{1,0:T(8,128)(2,1)} custom-call(bf16[4,576,128]{2,1,0:T(8,128)(2,1)} %bitcast.16, bf16[576,128]{1,0:T(8,128)(2,1)} %bitcast.19, bf16[16,576]{1,0:T(8,128)(2,1)} %refs_2_.1, s32[1]{0:T(128)S(6)} %copy.15.refs_3_, bf16[224,256]{1,0:T(8,128)(2,1)} %bitcast.21, f32[1,224]{1,0:T(1,128)} %bitcast.23, s32[8,4096]{1,0:T(8,128)} %bitcast.20, ...), custom_call_target="tpu_custom_call" | custom-call | tf_op jit(solution)/shard_map/pallas_call | solution.py:1103
  155.9 1.6 copy.16

commit v9 on v7

--- a/solution.py
+++ b/solution.py
@@ -567,7 +567,7 @@
         sems,
         lambda: visit(z),
         visit,
-        parts=4,
+        parts=2,
         after=after,
         delay=2,
         meanwhile=first,
@@ -1056,7 +1056,7 @@
         x_recv=dma((side, side)),
         y_send=dma((side, 2)),
         y_recv=dma((2, side)),
-        **dict(zip(("hs", "hr", "hts", "htr"), ring_sems(zs, 4))),
+        **dict(zip(("hs", "hr", "hts", "htr"), ring_sems(zs, 2))),
         pick=VMEM((peers * SRC_CAP, block), bf16),
         mix=VMEM((peers * SRC_CAP, block), bf16),
         pack=VMEM((cap, peers * SRC_CAP), bf16),

time: 156 us -> 156 us (level)
  no operation moved by 1% of the time
where the time goes in v9:
time: 156 us
  Pallas kernels  154 us (99%)
    pallas_call x1, Pallas kernels, local(): pl.pallas_call(functools.partial(layer_kernel, zs, peers, side, features,...  154 us

profile of v9, /device:TPU:1, one launch (start us, length us, event | category | flops | bytes accessed | tf_op | source)
XLA Modules:
  0.0 155.8 jit_solution(8482055959192414905)
XLA Ops:
  0.7 153.6 %shard_map.127 = bf16[224,256]{1,0:T(8,128)(2,1)} custom-call(bf16[4,576,128]{2,1,0:T(8,128)(2,1)} %bitcast.16, bf16[576,128]{1,0:T(8,128)(2,1)} %bitcast.19, bf16[16,576]{1,0:T(8,128)(2,1)} %refs_2_.1, s32[1]{0:T(128)S(6)} %copy.15.refs_3_, bf16[224,256]{1,0:T(8,128)(2,1)} %bitcast.21, f32[1,224]{1,0:T(1,128)} %bitcast.23, s32[8,4096]{1,0:T(8,128)} %bitcast.20, ...), custom_call_target="tpu_custom_call" | custom-call | tf_op jit(solution)/shard_map/pallas_call | solution.py:1097
  154.3 1.6 copy.16
